TPU v7x, 256 devices: a whole 4x4x8 slice. The times are simulated.
256 devices in a mesh: strip: 16 (over x, y_lo, core), vec: 16 (over y_hi, z).
Axes of the slice: x: 4, y: 4 (y_hi: 2, y_lo: 2; y = y_hi * 2 + y_lo), z: 8, core: 2. Of those that a mesh axis runs over, the one named last changes fastest.
Arguments:
- start_vectors: float32 [64, 512, 1024], P('vec', 'strip'), may hold values from -40 to 40
- potential: int32 [512, 1024], P('strip'), may hold values from 0 to 15
- bounds: int32 [4], replicated, may hold values from -96 to 96, as said below
Outputs:
- ortho_basis: float32 [64, 512, 1024], P('vec', 'strip')
- ritz_matrix: float32 [64, 64], replicated
Inputs may be any that keep to these rules, and one draw needn't show every extreme that they name: bounds[0] and bounds[1] enclose the spectrum of H: bounds[0] is at most -84 and bounds[1] at least 84; bounds[0] < bounds[2] < bounds[3] < bounds[1].
All inputs are finite; a program needn't handle non-finite values.
Results may differ from a plain program's by a relative error of at most 0.00021.
Values sent between devices are 32-bit elements; how exact they have to be, the bound alone decides.
A program may use at most 64 MiB of HBM per device.

v0:
```python
import math

import jax
import jax.numpy as jnp
from jax import lax
from jax.sharding import PartitionSpec as P

DEGREE = 32
POT_LEVELS = 16


grid_unit = 0.0625
disorder = 2.0


def extended(value, sides, width):
    for axis, dim in sides:
        count, length = (lax.axis_size(axis), value.shape[dim])
        up = [(i, (i + 1) % count) for i in range(count)]
        down = [(j, i) for i, j in up]
        last = lax.slice_in_dim(value, length - width, length, axis=dim)
        leading = lax.slice_in_dim(value, 0, width, axis=dim)
        before = lax.ppermute(last, axis, up)
        after = lax.ppermute(leading, axis, down)
        value = jnp.concatenate([before, value, after], axis=dim)
    return value


def filter_terms(bounds):
    edges = bounds.astype(jnp.float32) * grid_unit
    center = (edges[0] + edges[1]) * 0.5
    spread = (edges[1] - edges[0]) * 0.5
    theta_lo = jnp.arccos((edges[2] - center) / spread)
    theta_hi = jnp.arccos((edges[3] - center) / spread)
    orders = jnp.arange(1, DEGREE + 1).astype(jnp.float32)
    others = 2.0 * (jnp.sin(orders * theta_lo) - jnp.sin(orders * theta_hi)) / (orders * math.pi)
    first = jnp.reshape((theta_lo - theta_hi) / math.pi, (1,))
    return (jnp.concatenate([first, others]), center, spread)


def stencil(padded, pot_rows, center, spread):
    middle = padded[:, 1:-1]
    beside = padded[:, 2:] + padded[:, :-2] + jnp.roll(middle, 1, 2) + jnp.roll(middle, -1, 2)
    return ((pot_rows[None] - center) * middle - beside) / spread


def step_filter(start_vectors, pot_field, coeffs, center, spread):

    def advance(counter, carry):
        before, current, filtered = carry
        padded = extended(current, (("strip", 1),), 1)
        factor = jnp.where(counter == 0, 1.0, 2.0).astype(jnp.float32)
        after = factor * stencil(padded, pot_field, center, spread) - before
        return (current, after, filtered + coeffs[counter + 1] * after)

    initial = (jnp.zeros_like(start_vectors), start_vectors, coeffs[0] * start_vectors)
    return lax.fori_loop(0, DEGREE, advance, initial)[2]


def shards(start_vectors, potential, bounds):
    vec_local, rows, columns = start_vectors.shape
    pot_field = disorder * (potential.astype(jnp.float32) / (POT_LEVELS - 1) - 0.5)
    coeffs, center, spread = filter_terms(bounds)
    filtered = step_filter(start_vectors, pot_field, coeffs, center, spread)
    padded = extended(filtered, (("strip", 1),), 1)
    applied = stencil(padded, pot_field, 0.0, 1.0)
    slab_vecs, slab_applied = (
        lax.all_to_all(filtered, "vec", split_axis=1, concat_axis=0, tiled=True),
        lax.all_to_all(applied, "vec", split_axis=1, concat_axis=0, tiled=True),
    )
    total_vecs = slab_vecs.shape[0]
    y_rows = slab_vecs.reshape(total_vecs, -1)
    hy_rows = slab_applied.reshape(total_vecs, -1)
    gram_part = jnp.dot(
        y_rows, y_rows.T, precision=lax.Precision.HIGHEST, preferred_element_type=jnp.float32
    )
    cross_part = jnp.dot(
        y_rows, hy_rows.T, precision=lax.Precision.HIGHEST, preferred_element_type=jnp.float32
    )
    gram_sum, cross_sum = lax.psum((gram_part, cross_part), ("strip", "vec"))
    lower_factor = jnp.linalg.cholesky(gram_sum)
    site_count = lax.axis_size("strip") * rows * columns
    ortho = jax.scipy.linalg.solve_triangular(lower_factor, y_rows, lower=True)
    ortho_slab = (math.sqrt(site_count) * ortho).reshape(slab_vecs.shape)
    ortho_basis = lax.all_to_all(ortho_slab, "vec", split_axis=0, concat_axis=1, tiled=True)
    half_done = jax.scipy.linalg.solve_triangular(lower_factor, cross_sum, lower=True)
    ritz_matrix = float(rows) * jax.scipy.linalg.solve_triangular(
        lower_factor, half_done.T, lower=True
    )
    return (ortho_basis, ritz_matrix)


def solution(mesh):
    in_specs = (P("vec", "strip", None), P("strip", None), P())
    out_specs = (P("vec", "strip", None), P())
    return jax.shard_map(shards, mesh=mesh, in_specs=in_specs, out_specs=out_specs, check_vma=False)
```

profile of v0, /device:TPU:1, one launch (start us, length us, event | category | flops | bytes accessed | tf_op | source)
XLA Modules:
  0.0 382.5 jit_solution(7685637400722356539)
XLA Ops:
  6.6 212.7 %while.19 = (s32[]{:T(128)}, f32[4,32,1024]{2,1,0:T(8,128)S(1)}, f32[4,32,1024]{2,1,0:T(8,128)S(1)}, f32[4,32,1024]{2,1,0:T(8,128)S(1)}, f32[]{:T(128)}, /*index...) while((s32[]{:T(128)}, f32[4,32,1024]{2,1,0:T(8,128)S(1)}, ...), condition=%wide.region_1.2_spmd, body=%wide.region_0.1_spmd.sunk | while | flops 1867783 | bytes 8487209 | solution.py:57
  6.7 2.8 collective-permute-start
  11.0 1.6 collective-permute-done.1
  14.0 2.8 collective-permute-start.1
  19.1 4.4 %collective-permute-start.1 = (f32[4,1,1024]{2,1,0:T(1,128)S(1)}, f32[4,1,1024]{2,1,0:T(1,128)S(1)}, u32[]{:S(2)}, u32[]{:S(2)}) collective-permute-start(f32[4,1,1024]{2,1,0:T(1,128)S(1)} %get-tuple-element.300), channel_id=1, source_target_pairs={{16,0},{32,16},{48,32},{64,48},{80,64},{96,80},{112,96},{128,112},... | collective-permute-start | bytes 49160 | tf_op jit(solution)/shard_map/while/body/eval_jaxpr/ppermute | solution.py:24
  25.8 4.4 %collective-permute-start.1 = (f32[4,1,1024]{2,1,0:T(1,128)S(1)}, f32[4,1,1024]{2,1,0:T(1,128)S(1)}, u32[]{:S(2)}, u32[]{:S(2)}) collective-permute-start(f32[4,1,1024]{2,1,0:T(1,128)S(1)} %get-tuple-element.300), channel_id=1, source_target_pairs={{16,0},{32,16},{48,32},{64,48},{80,64},{96,80},{112,96},{128,112},... | collective-permute-start | bytes 49160 | tf_op jit(solution)/shard_map/while/body/eval_jaxpr/ppermute | solution.py:24
  32.4 4.4 %collective-permute-start.1 = (f32[4,1,1024]{2,1,0:T(1,128)S(1)}, f32[4,1,1024]{2,1,0:T(1,128)S(1)}, u32[]{:S(2)}, u32[]{:S(2)}) collective-permute-start(f32[4,1,1024]{2,1,0:T(1,128)S(1)} %get-tuple-element.300), channel_id=1, source_target_pairs={{16,0},{32,16},{48,32},{64,48},{80,64},{96,80},{112,96},{128,112},... | collective-permute-start | bytes 49160 | tf_op jit(solution)/shard_map/while/body/eval_jaxpr/ppermute | solution.py:24
  39.1 4.4 %collective-permute-start.1 = (f32[4,1,1024]{2,1,0:T(1,128)S(1)}, f32[4,1,1024]{2,1,0:T(1,128)S(1)}, u32[]{:S(2)}, u32[]{:S(2)}) collective-permute-start(f32[4,1,1024]{2,1,0:T(1,128)S(1)} %get-tuple-element.300), channel_id=1, source_target_pairs={{16,0},{32,16},{48,32},{64,48},{80,64},{96,80},{112,96},{128,112},... | collective-permute-start | bytes 49160 | tf_op jit(solution)/shard_map/while/body/eval_jaxpr/ppermute | solution.py:24
  45.8 4.4 %collective-permute-start.1 = (f32[4,1,1024]{2,1,0:T(1,128)S(1)}, f32[4,1,1024]{2,1,0:T(1,128)S(1)}, u32[]{:S(2)}, u32[]{:S(2)}) collective-permute-start(f32[4,1,1024]{2,1,0:T(1,128)S(1)} %get-tuple-element.300), channel_id=1, source_target_pairs={{16,0},{32,16},{48,32},{64,48},{80,64},{96,80},{112,96},{128,112},... | collective-permute-start | bytes 49160 | tf_op jit(solution)/shard_map/while/body/eval_jaxpr/ppermute | solution.py:24
  52.5 4.4 %collective-permute-start.1 = (f32[4,1,1024]{2,1,0:T(1,128)S(1)}, f32[4,1,1024]{2,1,0:T(1,128)S(1)}, u32[]{:S(2)}, u32[]{:S(2)}) collective-permute-start(f32[4,1,1024]{2,1,0:T(1,128)S(1)} %get-tuple-element.300), channel_id=1, source_target_pairs={{16,0},{32,16},{48,32},{64,48},{80,64},{96,80},{112,96},{128,112},... | collective-permute-start | bytes 49160 | tf_op jit(solution)/shard_map/while/body/eval_jaxpr/ppermute | solution.py:24
  59.2 4.4 %collective-permute-start.1 = (f32[4,1,1024]{2,1,0:T(1,128)S(1)}, f32[4,1,1024]{2,1,0:T(1,128)S(1)}, u32[]{:S(2)}, u32[]{:S(2)}) collective-permute-start(f32[4,1,1024]{2,1,0:T(1,128)S(1)} %get-tuple-element.300), channel_id=1, source_target_pairs={{16,0},{32,16},{48,32},{64,48},{80,64},{96,80},{112,96},{128,112},... | collective-permute-start | bytes 49160 | tf_op jit(solution)/shard_map/while/body/eval_jaxpr/ppermute | solution.py:24
  65.8 4.4 %collective-permute-start.1 = (f32[4,1,1024]{2,1,0:T(1,128)S(1)}, f32[4,1,1024]{2,1,0:T(1,128)S(1)}, u32[]{:S(2)}, u32[]{:S(2)}) collective-permute-start(f32[4,1,1024]{2,1,0:T(1,128)S(1)} %get-tuple-element.300), channel_id=1, source_target_pairs={{16,0},{32,16},{48,32},{64,48},{80,64},{96,80},{112,96},{128,112},... | collective-permute-start | bytes 49160 | tf_op jit(solution)/shard_map/while/body/eval_jaxpr/ppermute | solution.py:24
  72.5 4.4 %collective-permute-start.1 = (f32[4,1,1024]{2,1,0:T(1,128)S(1)}, f32[4,1,1024]{2,1,0:T(1,128)S(1)}, u32[]{:S(2)}, u32[]{:S(2)}) collective-permute-start(f32[4,1,1024]{2,1,0:T(1,128)S(1)} %get-tuple-element.300), channel_id=1, source_target_pairs={{16,0},{32,16},{48,32},{64,48},{80,64},{96,80},{112,96},{128,112},... | collective-permute-start | bytes 49160 | tf_op jit(solution)/shard_map/while/body/eval_jaxpr/ppermute | solution.py:24
  79.2 4.4 %collective-permute-start.1 = (f32[4,1,1024]{2,1,0:T(1,128)S(1)}, f32[4,1,1024]{2,1,0:T(1,128)S(1)}, u32[]{:S(2)}, u32[]{:S(2)}) collective-permute-start(f32[4,1,1024]{2,1,0:T(1,128)S(1)} %get-tuple-element.300), channel_id=1, source_target_pairs={{16,0},{32,16},{48,32},{64,48},{80,64},{96,80},{112,96},{128,112},... | collective-permute-start | bytes 49160 | tf_op jit(solution)/shard_map/while/body/eval_jaxpr/ppermute | solution.py:24
  85.9 4.4 %collective-permute-start.1 = (f32[4,1,1024]{2,1,0:T(1,128)S(1)}, f32[4,1,1024]{2,1,0:T(1,128)S(1)}, u32[]{:S(2)}, u32[]{:S(2)}) collective-permute-start(f32[4,1,1024]{2,1,0:T(1,128)S(1)} %get-tuple-element.300), channel_id=1, source_target_pairs={{16,0},{32,16},{48,32},{64,48},{80,64},{96,80},{112,96},{128,112},... | collective-permute-start | bytes 49160 | tf_op jit(solution)/shard_map/while/body/eval_jaxpr/ppermute | solution.py:24
  92.5 4.4 %collective-permute-start.1 = (f32[4,1,1024]{2,1,0:T(1,128)S(1)}, f32[4,1,1024]{2,1,0:T(1,128)S(1)}, u32[]{:S(2)}, u32[]{:S(2)}) collective-permute-start(f32[4,1,1024]{2,1,0:T(1,128)S(1)} %get-tuple-element.300), channel_id=1, source_target_pairs={{16,0},{32,16},{48,32},{64,48},{80,64},{96,80},{112,96},{128,112},... | collective-permute-start | bytes 49160 | tf_op jit(solution)/shard_map/while/body/eval_jaxpr/ppermute | solution.py:24
  99.2 4.4 %collective-permute-start.1 = (f32[4,1,1024]{2,1,0:T(1,128)S(1)}, f32[4,1,1024]{2,1,0:T(1,128)S(1)}, u32[]{:S(2)}, u32[]{:S(2)}) collective-permute-start(f32[4,1,1024]{2,1,0:T(1,128)S(1)} %get-tuple-element.300), channel_id=1, source_target_pairs={{16,0},{32,16},{48,32},{64,48},{80,64},{96,80},{112,96},{128,112},... | collective-permute-start | bytes 49160 | tf_op jit(solution)/shard_map/while/body/eval_jaxpr/ppermute | solution.py:24
  105.9 4.4 %collective-permute-start.1 = (f32[4,1,1024]{2,1,0:T(1,128)S(1)}, f32[4,1,1024]{2,1,0:T(1,128)S(1)}, u32[]{:S(2)}, u32[]{:S(2)}) collective-permute-start(f32[4,1,1024]{2,1,0:T(1,128)S(1)} %get-tuple-element.300), channel_id=1, source_target_pairs={{16,0},{32,16},{48,32},{64,48},{80,64},{96,80},{112,96},{128,112},... | collective-permute-start | bytes 49160 | tf_op jit(solution)/shard_map/while/body/eval_jaxpr/ppermute | solution.py:24
  112.6 4.4 %collective-permute-start.1 = (f32[4,1,1024]{2,1,0:T(1,128)S(1)}, f32[4,1,1024]{2,1,0:T(1,128)S(1)}, u32[]{:S(2)}, u32[]{:S(2)}) collective-permute-start(f32[4,1,1024]{2,1,0:T(1,128)S(1)} %get-tuple-element.300), channel_id=1, source_target_pairs={{16,0},{32,16},{48,32},{64,48},{80,64},{96,80},{112,96},{128,112},... | collective-permute-start | bytes 49160 | tf_op jit(solution)/shard_map/while/body/eval_jaxpr/ppermute | solution.py:24
  119.3 4.4 %collective-permute-start.1 = (f32[4,1,1024]{2,1,0:T(1,128)S(1)}, f32[4,1,1024]{2,1,0:T(1,128)S(1)}, u32[]{:S(2)}, u32[]{:S(2)}) collective-permute-start(f32[4,1,1024]{2,1,0:T(1,128)S(1)} %get-tuple-element.300), channel_id=1, source_target_pairs={{16,0},{32,16},{48,32},{64,48},{80,64},{96,80},{112,96},{128,112},... | collective-permute-start | bytes 49160 | tf_op jit(solution)/shard_map/while/body/eval_jaxpr/ppermute | solution.py:24
  125.9 4.4 %collective-permute-start.1 = (f32[4,1,1024]{2,1,0:T(1,128)S(1)}, f32[4,1,1024]{2,1,0:T(1,128)S(1)}, u32[]{:S(2)}, u32[]{:S(2)}) collective-permute-start(f32[4,1,1024]{2,1,0:T(1,128)S(1)} %get-tuple-element.300), channel_id=1, source_target_pairs={{16,0},{32,16},{48,32},{64,48},{80,64},{96,80},{112,96},{128,112},... | collective-permute-start | bytes 49160 | tf_op jit(solution)/shard_map/while/body/eval_jaxpr/ppermute | solution.py:24
  132.6 4.4 %collective-permute-start.1 = (f32[4,1,1024]{2,1,0:T(1,128)S(1)}, f32[4,1,1024]{2,1,0:T(1,128)S(1)}, u32[]{:S(2)}, u32[]{:S(2)}) collective-permute-start(f32[4,1,1024]{2,1,0:T(1,128)S(1)} %get-tuple-element.300), channel_id=1, source_target_pairs={{16,0},{32,16},{48,32},{64,48},{80,64},{96,80},{112,96},{128,112},... | collective-permute-start | bytes 49160 | tf_op jit(solution)/shard_map/while/body/eval_jaxpr/ppermute | solution.py:24
  139.3 4.4 %collective-permute-start.1 = (f32[4,1,1024]{2,1,0:T(1,128)S(1)}, f32[4,1,1024]{2,1,0:T(1,128)S(1)}, u32[]{:S(2)}, u32[]{:S(2)}) collective-permute-start(f32[4,1,1024]{2,1,0:T(1,128)S(1)} %get-tuple-element.300), channel_id=1, source_target_pairs={{16,0},{32,16},{48,32},{64,48},{80,64},{96,80},{112,96},{128,112},... | collective-permute-start | bytes 49160 | tf_op jit(solution)/shard_map/while/body/eval_jaxpr/ppermute | solution.py:24
  146.0 4.4 %collective-permute-start.1 = (f32[4,1,1024]{2,1,0:T(1,128)S(1)}, f32[4,1,1024]{2,1,0:T(1,128)S(1)}, u32[]{:S(2)}, u32[]{:S(2)}) collective-permute-start(f32[4,1,1024]{2,1,0:T(1,128)S(1)} %get-tuple-element.300), channel_id=1, source_target_pairs={{16,0},{32,16},{48,32},{64,48},{80,64},{96,80},{112,96},{128,112},... | collective-permute-start | bytes 49160 | tf_op jit(solution)/shard_map/while/body/eval_jaxpr/ppermute | solution.py:24
  152.6 4.4 %collective-permute-start.1 = (f32[4,1,1024]{2,1,0:T(1,128)S(1)}, f32[4,1,1024]{2,1,0:T(1,128)S(1)}, u32[]{:S(2)}, u32[]{:S(2)}) collective-permute-start(f32[4,1,1024]{2,1,0:T(1,128)S(1)} %get-tuple-element.300), channel_id=1, source_target_pairs={{16,0},{32,16},{48,32},{64,48},{80,64},{96,80},{112,96},{128,112},... | collective-permute-start | bytes 49160 | tf_op jit(solution)/shard_map/while/body/eval_jaxpr/ppermute | solution.py:24
  159.3 4.4 %collective-permute-start.1 = (f32[4,1,1024]{2,1,0:T(1,128)S(1)}, f32[4,1,1024]{2,1,0:T(1,128)S(1)}, u32[]{:S(2)}, u32[]{:S(2)}) collective-permute-start(f32[4,1,1024]{2,1,0:T(1,128)S(1)} %get-tuple-element.300), channel_id=1, source_target_pairs={{16,0},{32,16},{48,32},{64,48},{80,64},{96,80},{112,96},{128,112},... | collective-permute-start | bytes 49160 | tf_op jit(solution)/shard_map/while/body/eval_jaxpr/ppermute | solution.py:24
  166.0 4.4 %collective-permute-start.1 = (f32[4,1,1024]{2,1,0:T(1,128)S(1)}, f32[4,1,1024]{2,1,0:T(1,128)S(1)}, u32[]{:S(2)}, u32[]{:S(2)}) collective-permute-start(f32[4,1,1024]{2,1,0:T(1,128)S(1)} %get-tuple-element.300), channel_id=1, source_target_pairs={{16,0},{32,16},{48,32},{64,48},{80,64},{96,80},{112,96},{128,112},... | collective-permute-start | bytes 49160 | tf_op jit(solution)/shard_map/while/body/eval_jaxpr/ppermute | solution.py:24
  172.7 4.4 %collective-permute-start.1 = (f32[4,1,1024]{2,1,0:T(1,128)S(1)}, f32[4,1,1024]{2,1,0:T(1,128)S(1)}, u32[]{:S(2)}, u32[]{:S(2)}) collective-permute-start(f32[4,1,1024]{2,1,0:T(1,128)S(1)} %get-tuple-element.300), channel_id=1, source_target_pairs={{16,0},{32,16},{48,32},{64,48},{80,64},{96,80},{112,96},{128,112},... | collective-permute-start | bytes 49160 | tf_op jit(solution)/shard_map/while/body/eval_jaxpr/ppermute | solution.py:24
  179.4 4.4 %collective-permute-start.1 = (f32[4,1,1024]{2,1,0:T(1,128)S(1)}, f32[4,1,1024]{2,1,0:T(1,128)S(1)}, u32[]{:S(2)}, u32[]{:S(2)}) collective-permute-start(f32[4,1,1024]{2,1,0:T(1,128)S(1)} %get-tuple-element.300), channel_id=1, source_target_pairs={{16,0},{32,16},{48,32},{64,48},{80,64},{96,80},{112,96},{128,112},... | collective-permute-start | bytes 49160 | tf_op jit(solution)/shard_map/while/body/eval_jaxpr/ppermute | solution.py:24
  186.0 4.4 %collective-permute-start.1 = (f32[4,1,1024]{2,1,0:T(1,128)S(1)}, f32[4,1,1024]{2,1,0:T(1,128)S(1)}, u32[]{:S(2)}, u32[]{:S(2)}) collective-permute-start(f32[4,1,1024]{2,1,0:T(1,128)S(1)} %get-tuple-element.300), channel_id=1, source_target_pairs={{16,0},{32,16},{48,32},{64,48},{80,64},{96,80},{112,96},{128,112},... | collective-permute-start | bytes 49160 | tf_op jit(solution)/shard_map/while/body/eval_jaxpr/ppermute | solution.py:24
  192.7 4.4 %collective-permute-start.1 = (f32[4,1,1024]{2,1,0:T(1,128)S(1)}, f32[4,1,1024]{2,1,0:T(1,128)S(1)}, u32[]{:S(2)}, u32[]{:S(2)}) collective-permute-start(f32[4,1,1024]{2,1,0:T(1,128)S(1)} %get-tuple-element.300), channel_id=1, source_target_pairs={{16,0},{32,16},{48,32},{64,48},{80,64},{96,80},{112,96},{128,112},... | collective-permute-start | bytes 49160 | tf_op jit(solution)/shard_map/while/body/eval_jaxpr/ppermute | solution.py:24
  199.4 4.4 %collective-permute-start.1 = (f32[4,1,1024]{2,1,0:T(1,128)S(1)}, f32[4,1,1024]{2,1,0:T(1,128)S(1)}, u32[]{:S(2)}, u32[]{:S(2)}) collective-permute-start(f32[4,1,1024]{2,1,0:T(1,128)S(1)} %get-tuple-element.300), channel_id=1, source_target_pairs={{16,0},{32,16},{48,32},{64,48},{80,64},{96,80},{112,96},{128,112},... | collective-permute-start | bytes 49160 | tf_op jit(solution)/shard_map/while/body/eval_jaxpr/ppermute | solution.py:24
  206.1 4.4 %collective-permute-start.1 = (f32[4,1,1024]{2,1,0:T(1,128)S(1)}, f32[4,1,1024]{2,1,0:T(1,128)S(1)}, u32[]{:S(2)}, u32[]{:S(2)}) collective-permute-start(f32[4,1,1024]{2,1,0:T(1,128)S(1)} %get-tuple-element.300), channel_id=1, source_target_pairs={{16,0},{32,16},{48,32},{64,48},{80,64},{96,80},{112,96},{128,112},... | collective-permute-start | bytes 49160 | tf_op jit(solution)/shard_map/while/body/eval_jaxpr/ppermute | solution.py:24
  212.8 4.4 %collective-permute-start.1 = (f32[4,1,1024]{2,1,0:T(1,128)S(1)}, f32[4,1,1024]{2,1,0:T(1,128)S(1)}, u32[]{:S(2)}, u32[]{:S(2)}) collective-permute-start(f32[4,1,1024]{2,1,0:T(1,128)S(1)} %get-tuple-element.300), channel_id=1, source_target_pairs={{16,0},{32,16},{48,32},{64,48},{80,64},{96,80},{112,96},{128,112},... | collective-permute-start | bytes 49160 | tf_op jit(solution)/shard_map/while/body/eval_jaxpr/ppermute | solution.py:24
  219.3 1.1 copy.13
  220.4 9.1 %all-to-all-start = ((f32[4,32,1024]{2,0,1:T(4,128)}), f32[4,32,1024]{2,0,1:T(4,128)S(1)}, u32[]{:S(2)}, u32[]{:S(2)}) async-start(f32[4,32,1024]{2,0,1:T(4,128)} %copy.13), calls=%async_computation | async-start | bytes 1048576 | tf_op jit(solution)/shard_map/all_to_all | solution.py:68
  230.3 4.6 %collective-permute-start.2 = (f32[4,1,1024]{2,0,1:T(4,128)S(1)}, f32[4,1,1024]{2,0,1:T(4,128)S(1)}, u32[]{:S(2)}, u32[]{:S(2)}) collective-permute-start(f32[4,1,1024]{2,0,1:T(4,128)S(1)} %get-tuple-element.232), channel_id=1, source_target_pairs={{16,0},{32,16},{48,32},{64,48},{80,64},{96,80},{112,96},{128,112},... | collective-permute-start | bytes 49160 | tf_op jit(solution)/shard_map/ppermute | solution.py:24
  234.9 1.7 fusion.20
  238.5 3.1 fusion.10
  241.7 9.6 %all-to-all-start.2 = ((f32[4,32,1024]{2,0,1:T(4,128)}), f32[4,32,1024]{2,0,1:T(4,128)S(1)}, u32[]{:S(2)}, u32[]{:S(2)}) async-start(f32[4,32,1024]{2,0,1:T(4,128)} %fusion.10), calls=%async_computation.2 | async-start | bytes 1048576 | tf_op jit(solution)/shard_map/all_to_all | solution.py:69
  252.5 10.8 %all-to-all-done.2 = f32[4,32,1024]{2,0,1:T(4,128)S(1)} async-done(((f32[4,32,1024]{2,0,1:T(4,128)}), f32[4,32,1024]{2,0,1:T(4,128)S(1)}, u32[]{:S(2)}, u32[]{:S(2)}) %all-to-all-start.2) | async-done | bytes 524320 | tf_op jit(solution)/shard_map/all_to_all | solution.py:69
  264.4 82.5 %all-reduce = (f32[64,64]{0,1:T(8,128)S(1)}, f32[64,64]{1,0:T(8,128)S(1)}) all-reduce(f32[64,64]{0,1:T(8,128)S(1)} %fusion.24, f32[64,64]{1,0:T(8,128)S(1)} %fusion.25), channel_id=1, replica_groups=mesh['strip'=16,'vec'=16] {'strip','vec'}, use_global_device_ids=true, to_apply=%region_2.3 | all-reduce | flops 8192 | bytes 65536 | tf_op jit(solution)/shard_map/psum | solution.py:80
  347.1 5.8 %cholesky.16 = f32[64,64]{1,0:T(8,128)S(1)} custom-call(f32[64,64]{1,0:T(8,128)S(1)} %fusion.15), custom_call_target="Cholesky" | custom-call | tf_op jit(solution)/shard_map/jit(cholesky)/cholesky | solution.py:81
  354.2 4.9 %custom-call.10 = f32[1,64,64]{1,2,0:T(8,128)S(1)} custom-call(f32[1,64,64]{2,1,0:T(8,128)S(1)} %fusion.11), custom_call_target="InvertDiagBlocksLowerTriangular" | custom-call | tf_op jit(solution)/shard_map/jit(_solve_triangular)/triangular_solve | solution.py:83
  359.8 1.2 reshape.47
  361.0 5.2 %all-to-all-start.1 = ((f32[64,2,1024]{2,1,0:T(2,128)}), f32[64,2,1024]{2,1,0:T(2,128)S(1)}, u32[]{:S(2)}, u32[]{:S(2)}) async-start(f32[64,2,1024]{2,1,0:T(2,128)} %reshape.47), calls=%async_computation.1 | async-start | bytes 1048576 | tf_op jit(solution)/shard_map/all_to_all | solution.py:85
  367.3 14.0 %all-to-all-done.1 = f32[64,2,1024]{2,1,0:T(2,128)S(1)} async-done(((f32[64,2,1024]{2,1,0:T(2,128)}), f32[64,2,1024]{2,1,0:T(2,128)S(1)}, u32[]{:S(2)}, u32[]{:S(2)}) %all-to-all-start.1) | async-done | bytes 524320 | tf_op jit(solution)/shard_map/all_to_all | solution.py:85
  381.4 1.2 all_to_all.41
  (384 shorter events, 81.3 us)
Async XLA Ops:
  19.0 5.4 %collective-permute-start = (f32[4,1,1024]{2,1,0:T(1,128)S(1)}, f32[4,1,1024]{2,1,0:T(1,128)S(1)}, u32[]{:S(2)}, u32[]{:S(2)}) collective-permute-start(f32[4,1,1024]{2,1,0:T(1,128)S(1)} %get-tuple-element.299), channel_id=1, source_target_pairs={{0,16},{16,32},{32,48},{48,64},{64,80},{80,96},{96,112},{112,128},... | collective-permute-start | bytes 49160 | tf_op jit(solution)/shard_map/while/body/eval_jaxpr/ppermute | solution.py:23
  25.7 5.4 %collective-permute-start = (f32[4,1,1024]{2,1,0:T(1,128)S(1)}, f32[4,1,1024]{2,1,0:T(1,128)S(1)}, u32[]{:S(2)}, u32[]{:S(2)}) collective-permute-start(f32[4,1,1024]{2,1,0:T(1,128)S(1)} %get-tuple-element.299), channel_id=1, source_target_pairs={{0,16},{16,32},{32,48},{48,64},{64,80},{80,96},{96,112},{112,128},... | collective-permute-start | bytes 49160 | tf_op jit(solution)/shard_map/while/body/eval_jaxpr/ppermute | solution.py:23
  32.3 5.4 %collective-permute-start = (f32[4,1,1024]{2,1,0:T(1,128)S(1)}, f32[4,1,1024]{2,1,0:T(1,128)S(1)}, u32[]{:S(2)}, u32[]{:S(2)}) collective-permute-start(f32[4,1,1024]{2,1,0:T(1,128)S(1)} %get-tuple-element.299), channel_id=1, source_target_pairs={{0,16},{16,32},{32,48},{48,64},{64,80},{80,96},{96,112},{112,128},... | collective-permute-start | bytes 49160 | tf_op jit(solution)/shard_map/while/body/eval_jaxpr/ppermute | solution.py:23
  32.4 5.3 %collective-permute-start.1 = (f32[4,1,1024]{2,1,0:T(1,128)S(1)}, f32[4,1,1024]{2,1,0:T(1,128)S(1)}, u32[]{:S(2)}, u32[]{:S(2)}) collective-permute-start(f32[4,1,1024]{2,1,0:T(1,128)S(1)} %get-tuple-element.300), channel_id=1, source_target_pairs={{16,0},{32,16},{48,32},{64,48},{80,64},{96,80},{112,96},{128,112},... | collective-permute-start | bytes 49160 | tf_op jit(solution)/shard_map/while/body/eval_jaxpr/ppermute | solution.py:24
  39.0 5.4 %collective-permute-start = (f32[4,1,1024]{2,1,0:T(1,128)S(1)}, f32[4,1,1024]{2,1,0:T(1,128)S(1)}, u32[]{:S(2)}, u32[]{:S(2)}) collective-permute-start(f32[4,1,1024]{2,1,0:T(1,128)S(1)} %get-tuple-element.299), channel_id=1, source_target_pairs={{0,16},{16,32},{32,48},{48,64},{64,80},{80,96},{96,112},{112,128},... | collective-permute-start | bytes 49160 | tf_op jit(solution)/shard_map/while/body/eval_jaxpr/ppermute | solution.py:23
  39.1 5.3 %collective-permute-start.1 = (f32[4,1,1024]{2,1,0:T(1,128)S(1)}, f32[4,1,1024]{2,1,0:T(1,128)S(1)}, u32[]{:S(2)}, u32[]{:S(2)}) collective-permute-start(f32[4,1,1024]{2,1,0:T(1,128)S(1)} %get-tuple-element.300), channel_id=1, source_target_pairs={{16,0},{32,16},{48,32},{64,48},{80,64},{96,80},{112,96},{128,112},... | collective-permute-start | bytes 49160 | tf_op jit(solution)/shard_map/while/body/eval_jaxpr/ppermute | solution.py:24
  45.7 5.4 %collective-permute-start = (f32[4,1,1024]{2,1,0:T(1,128)S(1)}, f32[4,1,1024]{2,1,0:T(1,128)S(1)}, u32[]{:S(2)}, u32[]{:S(2)}) collective-permute-start(f32[4,1,1024]{2,1,0:T(1,128)S(1)} %get-tuple-element.299), channel_id=1, source_target_pairs={{0,16},{16,32},{32,48},{48,64},{64,80},{80,96},{96,112},{112,128},... | collective-permute-start | bytes 49160 | tf_op jit(solution)/shard_map/while/body/eval_jaxpr/ppermute | solution.py:23
  45.8 5.3 %collective-permute-start.1 = (f32[4,1,1024]{2,1,0:T(1,128)S(1)}, f32[4,1,1024]{2,1,0:T(1,128)S(1)}, u32[]{:S(2)}, u32[]{:S(2)}) collective-permute-start(f32[4,1,1024]{2,1,0:T(1,128)S(1)} %get-tuple-element.300), channel_id=1, source_target_pairs={{16,0},{32,16},{48,32},{64,48},{80,64},{96,80},{112,96},{128,112},... | collective-permute-start | bytes 49160 | tf_op jit(solution)/shard_map/while/body/eval_jaxpr/ppermute | solution.py:24
  52.4 5.4 %collective-permute-start = (f32[4,1,1024]{2,1,0:T(1,128)S(1)}, f32[4,1,1024]{2,1,0:T(1,128)S(1)}, u32[]{:S(2)}, u32[]{:S(2)}) collective-permute-start(f32[4,1,1024]{2,1,0:T(1,128)S(1)} %get-tuple-element.299), channel_id=1, source_target_pairs={{0,16},{16,32},{32,48},{48,64},{64,80},{80,96},{96,112},{112,128},... | collective-permute-start | bytes 49160 | tf_op jit(solution)/shard_map/while/body/eval_jaxpr/ppermute | solution.py:23
  52.5 5.3 %collective-permute-start.1 = (f32[4,1,1024]{2,1,0:T(1,128)S(1)}, f32[4,1,1024]{2,1,0:T(1,128)S(1)}, u32[]{:S(2)}, u32[]{:S(2)}) collective-permute-start(f32[4,1,1024]{2,1,0:T(1,128)S(1)} %get-tuple-element.300), channel_id=1, source_target_pairs={{16,0},{32,16},{48,32},{64,48},{80,64},{96,80},{112,96},{128,112},... | collective-permute-start | bytes 49160 | tf_op jit(solution)/shard_map/while/body/eval_jaxpr/ppermute | solution.py:24
  59.1 5.4 %collective-permute-start = (f32[4,1,1024]{2,1,0:T(1,128)S(1)}, f32[4,1,1024]{2,1,0:T(1,128)S(1)}, u32[]{:S(2)}, u32[]{:S(2)}) collective-permute-start(f32[4,1,1024]{2,1,0:T(1,128)S(1)} %get-tuple-element.299), channel_id=1, source_target_pairs={{0,16},{16,32},{32,48},{48,64},{64,80},{80,96},{96,112},{112,128},... | collective-permute-start | bytes 49160 | tf_op jit(solution)/shard_map/while/body/eval_jaxpr/ppermute | solution.py:23
  59.2 5.3 %collective-permute-start.1 = (f32[4,1,1024]{2,1,0:T(1,128)S(1)}, f32[4,1,1024]{2,1,0:T(1,128)S(1)}, u32[]{:S(2)}, u32[]{:S(2)}) collective-permute-start(f32[4,1,1024]{2,1,0:T(1,128)S(1)} %get-tuple-element.300), channel_id=1, source_target_pairs={{16,0},{32,16},{48,32},{64,48},{80,64},{96,80},{112,96},{128,112},... | collective-permute-start | bytes 49160 | tf_op jit(solution)/shard_map/while/body/eval_jaxpr/ppermute | solution.py:24
  65.7 5.4 %collective-permute-start = (f32[4,1,1024]{2,1,0:T(1,128)S(1)}, f32[4,1,1024]{2,1,0:T(1,128)S(1)}, u32[]{:S(2)}, u32[]{:S(2)}) collective-permute-start(f32[4,1,1024]{2,1,0:T(1,128)S(1)} %get-tuple-element.299), channel_id=1, source_target_pairs={{0,16},{16,32},{32,48},{48,64},{64,80},{80,96},{96,112},{112,128},... | collective-permute-start | bytes 49160 | tf_op jit(solution)/shard_map/while/body/eval_jaxpr/ppermute | solution.py:23
  65.8 5.3 %collective-permute-start.1 = (f32[4,1,1024]{2,1,0:T(1,128)S(1)}, f32[4,1,1024]{2,1,0:T(1,128)S(1)}, u32[]{:S(2)}, u32[]{:S(2)}) collective-permute-start(f32[4,1,1024]{2,1,0:T(1,128)S(1)} %get-tuple-element.300), channel_id=1, source_target_pairs={{16,0},{32,16},{48,32},{64,48},{80,64},{96,80},{112,96},{128,112},... | collective-permute-start | bytes 49160 | tf_op jit(solution)/shard_map/while/body/eval_jaxpr/ppermute | solution.py:24
  72.4 5.4 %collective-permute-start = (f32[4,1,1024]{2,1,0:T(1,128)S(1)}, f32[4,1,1024]{2,1,0:T(1,128)S(1)}, u32[]{:S(2)}, u32[]{:S(2)}) collective-permute-start(f32[4,1,1024]{2,1,0:T(1,128)S(1)} %get-tuple-element.299), channel_id=1, source_target_pairs={{0,16},{16,32},{32,48},{48,64},{64,80},{80,96},{96,112},{112,128},... | collective-permute-start | bytes 49160 | tf_op jit(solution)/shard_map/while/body/eval_jaxpr/ppermute | solution.py:23
  72.5 5.3 %collective-permute-start.1 = (f32[4,1,1024]{2,1,0:T(1,128)S(1)}, f32[4,1,1024]{2,1,0:T(1,128)S(1)}, u32[]{:S(2)}, u32[]{:S(2)}) collective-permute-start(f32[4,1,1024]{2,1,0:T(1,128)S(1)} %get-tuple-element.300), channel_id=1, source_target_pairs={{16,0},{32,16},{48,32},{64,48},{80,64},{96,80},{112,96},{128,112},... | collective-permute-start | bytes 49160 | tf_op jit(solution)/shard_map/while/body/eval_jaxpr/ppermute | solution.py:24
  79.1 5.4 %collective-permute-start = (f32[4,1,1024]{2,1,0:T(1,128)S(1)}, f32[4,1,1024]{2,1,0:T(1,128)S(1)}, u32[]{:S(2)}, u32[]{:S(2)}) collective-permute-start(f32[4,1,1024]{2,1,0:T(1,128)S(1)} %get-tuple-element.299), channel_id=1, source_target_pairs={{0,16},{16,32},{32,48},{48,64},{64,80},{80,96},{96,112},{112,128},... | collective-permute-start | bytes 49160 | tf_op jit(solution)/shard_map/while/body/eval_jaxpr/ppermute | solution.py:23
  79.2 5.3 %collective-permute-start.1 = (f32[4,1,1024]{2,1,0:T(1,128)S(1)}, f32[4,1,1024]{2,1,0:T(1,128)S(1)}, u32[]{:S(2)}, u32[]{:S(2)}) collective-permute-start(f32[4,1,1024]{2,1,0:T(1,128)S(1)} %get-tuple-element.300), channel_id=1, source_target_pairs={{16,0},{32,16},{48,32},{64,48},{80,64},{96,80},{112,96},{128,112},... | collective-permute-start | bytes 49160 | tf_op jit(solution)/shard_map/while/body/eval_jaxpr/ppermute | solution.py:24
  85.8 5.4 %collective-permute-start = (f32[4,1,1024]{2,1,0:T(1,128)S(1)}, f32[4,1,1024]{2,1,0:T(1,128)S(1)}, u32[]{:S(2)}, u32[]{:S(2)}) collective-permute-start(f32[4,1,1024]{2,1,0:T(1,128)S(1)} %get-tuple-element.299), channel_id=1, source_target_pairs={{0,16},{16,32},{32,48},{48,64},{64,80},{80,96},{96,112},{112,128},... | collective-permute-start | bytes 49160 | tf_op jit(solution)/shard_map/while/body/eval_jaxpr/ppermute | solution.py:23
  85.9 5.3 %collective-permute-start.1 = (f32[4,1,1024]{2,1,0:T(1,128)S(1)}, f32[4,1,1024]{2,1,0:T(1,128)S(1)}, u32[]{:S(2)}, u32[]{:S(2)}) collective-permute-start(f32[4,1,1024]{2,1,0:T(1,128)S(1)} %get-tuple-element.300), channel_id=1, source_target_pairs={{16,0},{32,16},{48,32},{64,48},{80,64},{96,80},{112,96},{128,112},... | collective-permute-start | bytes 49160 | tf_op jit(solution)/shard_map/while/body/eval_jaxpr/ppermute | solution.py:24
  92.5 5.4 %collective-permute-start = (f32[4,1,1024]{2,1,0:T(1,128)S(1)}, f32[4,1,1024]{2,1,0:T(1,128)S(1)}, u32[]{:S(2)}, u32[]{:S(2)}) collective-permute-start(f32[4,1,1024]{2,1,0:T(1,128)S(1)} %get-tuple-element.299), channel_id=1, source_target_pairs={{0,16},{16,32},{32,48},{48,64},{64,80},{80,96},{96,112},{112,128},... | collective-permute-start | bytes 49160 | tf_op jit(solution)/shard_map/while/body/eval_jaxpr/ppermute | solution.py:23
  92.5 5.3 %collective-permute-start.1 = (f32[4,1,1024]{2,1,0:T(1,128)S(1)}, f32[4,1,1024]{2,1,0:T(1,128)S(1)}, u32[]{:S(2)}, u32[]{:S(2)}) collective-permute-start(f32[4,1,1024]{2,1,0:T(1,128)S(1)} %get-tuple-element.300), channel_id=1, source_target_pairs={{16,0},{32,16},{48,32},{64,48},{80,64},{96,80},{112,96},{128,112},... | collective-permute-start | bytes 49160 | tf_op jit(solution)/shard_map/while/body/eval_jaxpr/ppermute | solution.py:24
  99.1 5.4 %collective-permute-start = (f32[4,1,1024]{2,1,0:T(1,128)S(1)}, f32[4,1,1024]{2,1,0:T(1,128)S(1)}, u32[]{:S(2)}, u32[]{:S(2)}) collective-permute-start(f32[4,1,1024]{2,1,0:T(1,128)S(1)} %get-tuple-element.299), channel_id=1, source_target_pairs={{0,16},{16,32},{32,48},{48,64},{64,80},{80,96},{96,112},{112,128},... | collective-permute-start | bytes 49160 | tf_op jit(solution)/shard_map/while/body/eval_jaxpr/ppermute | solution.py:23
  99.2 5.3 %collective-permute-start.1 = (f32[4,1,1024]{2,1,0:T(1,128)S(1)}, f32[4,1,1024]{2,1,0:T(1,128)S(1)}, u32[]{:S(2)}, u32[]{:S(2)}) collective-permute-start(f32[4,1,1024]{2,1,0:T(1,128)S(1)} %get-tuple-element.300), channel_id=1, source_target_pairs={{16,0},{32,16},{48,32},{64,48},{80,64},{96,80},{112,96},{128,112},... | collective-permute-start | bytes 49160 | tf_op jit(solution)/shard_map/while/body/eval_jaxpr/ppermute | solution.py:24
  105.8 5.4 %collective-permute-start = (f32[4,1,1024]{2,1,0:T(1,128)S(1)}, f32[4,1,1024]{2,1,0:T(1,128)S(1)}, u32[]{:S(2)}, u32[]{:S(2)}) collective-permute-start(f32[4,1,1024]{2,1,0:T(1,128)S(1)} %get-tuple-element.299), channel_id=1, source_target_pairs={{0,16},{16,32},{32,48},{48,64},{64,80},{80,96},{96,112},{112,128},... | collective-permute-start | bytes 49160 | tf_op jit(solution)/shard_map/while/body/eval_jaxpr/ppermute | solution.py:23
  105.9 5.3 %collective-permute-start.1 = (f32[4,1,1024]{2,1,0:T(1,128)S(1)}, f32[4,1,1024]{2,1,0:T(1,128)S(1)}, u32[]{:S(2)}, u32[]{:S(2)}) collective-permute-start(f32[4,1,1024]{2,1,0:T(1,128)S(1)} %get-tuple-element.300), channel_id=1, source_target_pairs={{16,0},{32,16},{48,32},{64,48},{80,64},{96,80},{112,96},{128,112},... | collective-permute-start | bytes 49160 | tf_op jit(solution)/shard_map/while/body/eval_jaxpr/ppermute | solution.py:24
  112.5 5.4 %collective-permute-start = (f32[4,1,1024]{2,1,0:T(1,128)S(1)}, f32[4,1,1024]{2,1,0:T(1,128)S(1)}, u32[]{:S(2)}, u32[]{:S(2)}) collective-permute-start(f32[4,1,1024]{2,1,0:T(1,128)S(1)} %get-tuple-element.299), channel_id=1, source_target_pairs={{0,16},{16,32},{32,48},{48,64},{64,80},{80,96},{96,112},{112,128},... | collective-permute-start | bytes 49160 | tf_op jit(solution)/shard_map/while/body/eval_jaxpr/ppermute | solution.py:23
  112.6 5.3 %collective-permute-start.1 = (f32[4,1,1024]{2,1,0:T(1,128)S(1)}, f32[4,1,1024]{2,1,0:T(1,128)S(1)}, u32[]{:S(2)}, u32[]{:S(2)}) collective-permute-start(f32[4,1,1024]{2,1,0:T(1,128)S(1)} %get-tuple-element.300), channel_id=1, source_target_pairs={{16,0},{32,16},{48,32},{64,48},{80,64},{96,80},{112,96},{128,112},... | collective-permute-start | bytes 49160 | tf_op jit(solution)/shard_map/while/body/eval_jaxpr/ppermute | solution.py:24
  119.2 5.4 %collective-permute-start = (f32[4,1,1024]{2,1,0:T(1,128)S(1)}, f32[4,1,1024]{2,1,0:T(1,128)S(1)}, u32[]{:S(2)}, u32[]{:S(2)}) collective-permute-start(f32[4,1,1024]{2,1,0:T(1,128)S(1)} %get-tuple-element.299), channel_id=1, source_target_pairs={{0,16},{16,32},{32,48},{48,64},{64,80},{80,96},{96,112},{112,128},... | collective-permute-start | bytes 49160 | tf_op jit(solution)/shard_map/while/body/eval_jaxpr/ppermute | solution.py:23
  125.8 5.4 %collective-permute-start = (f32[4,1,1024]{2,1,0:T(1,128)S(1)}, f32[4,1,1024]{2,1,0:T(1,128)S(1)}, u32[]{:S(2)}, u32[]{:S(2)}) collective-permute-start(f32[4,1,1024]{2,1,0:T(1,128)S(1)} %get-tuple-element.299), channel_id=1, source_target_pairs={{0,16},{16,32},{32,48},{48,64},{64,80},{80,96},{96,112},{112,128},... | collective-permute-start | bytes 49160 | tf_op jit(solution)/shard_map/while/body/eval_jaxpr/ppermute | solution.py:23
  132.5 5.4 %collective-permute-start = (f32[4,1,1024]{2,1,0:T(1,128)S(1)}, f32[4,1,1024]{2,1,0:T(1,128)S(1)}, u32[]{:S(2)}, u32[]{:S(2)}) collective-permute-start(f32[4,1,1024]{2,1,0:T(1,128)S(1)} %get-tuple-element.299), channel_id=1, source_target_pairs={{0,16},{16,32},{32,48},{48,64},{64,80},{80,96},{96,112},{112,128},... | collective-permute-start | bytes 49160 | tf_op jit(solution)/shard_map/while/body/eval_jaxpr/ppermute | solution.py:23
  139.2 5.4 %collective-permute-start = (f32[4,1,1024]{2,1,0:T(1,128)S(1)}, f32[4,1,1024]{2,1,0:T(1,128)S(1)}, u32[]{:S(2)}, u32[]{:S(2)}) collective-permute-start(f32[4,1,1024]{2,1,0:T(1,128)S(1)} %get-tuple-element.299), channel_id=1, source_target_pairs={{0,16},{16,32},{32,48},{48,64},{64,80},{80,96},{96,112},{112,128},... | collective-permute-start | bytes 49160 | tf_op jit(solution)/shard_map/while/body/eval_jaxpr/ppermute | solution.py:23
  145.9 5.4 %collective-permute-start = (f32[4,1,1024]{2,1,0:T(1,128)S(1)}, f32[4,1,1024]{2,1,0:T(1,128)S(1)}, u32[]{:S(2)}, u32[]{:S(2)}) collective-permute-start(f32[4,1,1024]{2,1,0:T(1,128)S(1)} %get-tuple-element.299), channel_id=1, source_target_pairs={{0,16},{16,32},{32,48},{48,64},{64,80},{80,96},{96,112},{112,128},... | collective-permute-start | bytes 49160 | tf_op jit(solution)/shard_map/while/body/eval_jaxpr/ppermute | solution.py:23
  152.6 5.4 %collective-permute-start = (f32[4,1,1024]{2,1,0:T(1,128)S(1)}, f32[4,1,1024]{2,1,0:T(1,128)S(1)}, u32[]{:S(2)}, u32[]{:S(2)}) collective-permute-start(f32[4,1,1024]{2,1,0:T(1,128)S(1)} %get-tuple-element.299), channel_id=1, source_target_pairs={{0,16},{16,32},{32,48},{48,64},{64,80},{80,96},{96,112},{112,128},... | collective-permute-start | bytes 49160 | tf_op jit(solution)/shard_map/while/body/eval_jaxpr/ppermute | solution.py:23
  159.2 5.4 %collective-permute-start = (f32[4,1,1024]{2,1,0:T(1,128)S(1)}, f32[4,1,1024]{2,1,0:T(1,128)S(1)}, u32[]{:S(2)}, u32[]{:S(2)}) collective-permute-start(f32[4,1,1024]{2,1,0:T(1,128)S(1)} %get-tuple-element.299), channel_id=1, source_target_pairs={{0,16},{16,32},{32,48},{48,64},{64,80},{80,96},{96,112},{112,128},... | collective-permute-start | bytes 49160 | tf_op jit(solution)/shard_map/while/body/eval_jaxpr/ppermute | solution.py:23
  159.3 5.3 %collective-permute-start.1 = (f32[4,1,1024]{2,1,0:T(1,128)S(1)}, f32[4,1,1024]{2,1,0:T(1,128)S(1)}, u32[]{:S(2)}, u32[]{:S(2)}) collective-permute-start(f32[4,1,1024]{2,1,0:T(1,128)S(1)} %get-tuple-element.300), channel_id=1, source_target_pairs={{16,0},{32,16},{48,32},{64,48},{80,64},{96,80},{112,96},{128,112},... | collective-permute-start | bytes 49160 | tf_op jit(solution)/shard_map/while/body/eval_jaxpr/ppermute | solution.py:24
  165.9 5.4 %collective-permute-start = (f32[4,1,1024]{2,1,0:T(1,128)S(1)}, f32[4,1,1024]{2,1,0:T(1,128)S(1)}, u32[]{:S(2)}, u32[]{:S(2)}) collective-permute-start(f32[4,1,1024]{2,1,0:T(1,128)S(1)} %get-tuple-element.299), channel_id=1, source_target_pairs={{0,16},{16,32},{32,48},{48,64},{64,80},{80,96},{96,112},{112,128},... | collective-permute-start | bytes 49160 | tf_op jit(solution)/shard_map/while/body/eval_jaxpr/ppermute | solution.py:23
  172.6 5.4 %collective-permute-start = (f32[4,1,1024]{2,1,0:T(1,128)S(1)}, f32[4,1,1024]{2,1,0:T(1,128)S(1)}, u32[]{:S(2)}, u32[]{:S(2)}) collective-permute-start(f32[4,1,1024]{2,1,0:T(1,128)S(1)} %get-tuple-element.299), channel_id=1, source_target_pairs={{0,16},{16,32},{32,48},{48,64},{64,80},{80,96},{96,112},{112,128},... | collective-permute-start | bytes 49160 | tf_op jit(solution)/shard_map/while/body/eval_jaxpr/ppermute | solution.py:23
  179.3 5.4 %collective-permute-start = (f32[4,1,1024]{2,1,0:T(1,128)S(1)}, f32[4,1,1024]{2,1,0:T(1,128)S(1)}, u32[]{:S(2)}, u32[]{:S(2)}) collective-permute-start(f32[4,1,1024]{2,1,0:T(1,128)S(1)} %get-tuple-element.299), channel_id=1, source_target_pairs={{0,16},{16,32},{32,48},{48,64},{64,80},{80,96},{96,112},{112,128},... | collective-permute-start | bytes 49160 | tf_op jit(solution)/shard_map/while/body/eval_jaxpr/ppermute | solution.py:23
  185.9 5.4 %collective-permute-start = (f32[4,1,1024]{2,1,0:T(1,128)S(1)}, f32[4,1,1024]{2,1,0:T(1,128)S(1)}, u32[]{:S(2)}, u32[]{:S(2)}) collective-permute-start(f32[4,1,1024]{2,1,0:T(1,128)S(1)} %get-tuple-element.299), channel_id=1, source_target_pairs={{0,16},{16,32},{32,48},{48,64},{64,80},{80,96},{96,112},{112,128},... | collective-permute-start | bytes 49160 | tf_op jit(solution)/shard_map/while/body/eval_jaxpr/ppermute | solution.py:23
  192.6 5.4 %collective-permute-start = (f32[4,1,1024]{2,1,0:T(1,128)S(1)}, f32[4,1,1024]{2,1,0:T(1,128)S(1)}, u32[]{:S(2)}, u32[]{:S(2)}) collective-permute-start(f32[4,1,1024]{2,1,0:T(1,128)S(1)} %get-tuple-element.299), channel_id=1, source_target_pairs={{0,16},{16,32},{32,48},{48,64},{64,80},{80,96},{96,112},{112,128},... | collective-permute-start | bytes 49160 | tf_op jit(solution)/shard_map/while/body/eval_jaxpr/ppermute | solution.py:23
  199.3 5.4 %collective-permute-start = (f32[4,1,1024]{2,1,0:T(1,128)S(1)}, f32[4,1,1024]{2,1,0:T(1,128)S(1)}, u32[]{:S(2)}, u32[]{:S(2)}) collective-permute-start(f32[4,1,1024]{2,1,0:T(1,128)S(1)} %get-tuple-element.299), channel_id=1, source_target_pairs={{0,16},{16,32},{32,48},{48,64},{64,80},{80,96},{96,112},{112,128},... | collective-permute-start | bytes 49160 | tf_op jit(solution)/shard_map/while/body/eval_jaxpr/ppermute | solution.py:23
  206.0 5.4 %collective-permute-start = (f32[4,1,1024]{2,1,0:T(1,128)S(1)}, f32[4,1,1024]{2,1,0:T(1,128)S(1)}, u32[]{:S(2)}, u32[]{:S(2)}) collective-permute-start(f32[4,1,1024]{2,1,0:T(1,128)S(1)} %get-tuple-element.299), channel_id=1, source_target_pairs={{0,16},{16,32},{32,48},{48,64},{64,80},{80,96},{96,112},{112,128},... | collective-permute-start | bytes 49160 | tf_op jit(solution)/shard_map/while/body/eval_jaxpr/ppermute | solution.py:23
  212.7 5.4 %collective-permute-start = (f32[4,1,1024]{2,1,0:T(1,128)S(1)}, f32[4,1,1024]{2,1,0:T(1,128)S(1)}, u32[]{:S(2)}, u32[]{:S(2)}) collective-permute-start(f32[4,1,1024]{2,1,0:T(1,128)S(1)} %get-tuple-element.299), channel_id=1, source_target_pairs={{0,16},{16,32},{32,48},{48,64},{64,80},{80,96},{96,112},{112,128},... | collective-permute-start | bytes 49160 | tf_op jit(solution)/shard_map/while/body/eval_jaxpr/ppermute | solution.py:23
  220.4 21.2 %all-to-all-start = ((f32[4,32,1024]{2,0,1:T(4,128)}), f32[4,32,1024]{2,0,1:T(4,128)S(1)}, u32[]{:S(2)}, u32[]{:S(2)}) async-start(f32[4,32,1024]{2,0,1:T(4,128)} %copy.13), calls=%async_computation | async-start | bytes 1048576 | tf_op jit(solution)/shard_map/all_to_all | solution.py:68
  230.3 7.3 %collective-permute-start.2 = (f32[4,1,1024]{2,0,1:T(4,128)S(1)}, f32[4,1,1024]{2,0,1:T(4,128)S(1)}, u32[]{:S(2)}, u32[]{:S(2)}) collective-permute-start(f32[4,1,1024]{2,0,1:T(4,128)S(1)} %get-tuple-element.232), channel_id=1, source_target_pairs={{16,0},{32,16},{48,32},{64,48},{80,64},{96,80},{112,96},{128,112},... | collective-permute-start | bytes 49160 | tf_op jit(solution)/shard_map/ppermute | solution.py:24
  241.7 21.6 %all-to-all-start.2 = ((f32[4,32,1024]{2,0,1:T(4,128)}), f32[4,32,1024]{2,0,1:T(4,128)S(1)}, u32[]{:S(2)}, u32[]{:S(2)}) async-start(f32[4,32,1024]{2,0,1:T(4,128)} %fusion.10), calls=%async_computation.2 | async-start | bytes 1048576 | tf_op jit(solution)/shard_map/all_to_all | solution.py:69
  361.0 20.3 %all-to-all-start.1 = ((f32[64,2,1024]{2,1,0:T(2,128)}), f32[64,2,1024]{2,1,0:T(2,128)S(1)}, u32[]{:S(2)}, u32[]{:S(2)}) async-start(f32[64,2,1024]{2,1,0:T(2,128)} %reshape.47), calls=%async_computation.1 | async-start | bytes 1048576 | tf_op jit(solution)/shard_map/all_to_all | solution.py:85
  (23 other events, 111.2 us)
where the time goes:
time: 384 us; the launch traced here: 383 us
  starting transfers between devices  170 us (44%)
  blocking collectives  82.5 us (21%)
  other arithmetic  50.9 us (13%)
  local copies, waits for them, and re-layouts  42 us (11%)
  waiting for transfers between devices  27.7 us (7%)
  between operations  4.84 us (1%)
    ppermute x33, starting transfers between devices, extended(): after = lax.ppermute(leading, axis, down)  141 us
    psum x1, blocking collectives, shards(): gram_sum, cross_sum = lax.psum((gram_part, cross_part), ('strip', 'vec'))  82.5 us
    add x32, other arithmetic, advance(): return (current, after, filtered + coeffs[counter + 1] * after)  35.1 us
    dynamic_slice x32, local copies, waits for them, and re-layouts, advance(): return (current, after, filtered + coeffs[counter + 1] * after)  19.9 us
    all_to_all x1, waiting for transfers between devices, shards(): lax.all_to_all(ortho_slab, 'vec', split_axis=0, concat_axis=1, tiled=True)  14 us
    all_to_all x1, waiting for transfers between devices, shards(): lax.all_to_all(applied, 'vec', split_axis=1, concat_axis=0, tiled=True)  10.8 us
    all_to_all x1, starting transfers between devices, shards(): lax.all_to_all(applied, 'vec', split_axis=1, concat_axis=0, tiled=True)  9.64 us
    all_to_all x1, starting transfers between devices, shards(): lax.all_to_all(filtered, 'vec', split_axis=1, concat_axis=0, tiled=True)  9.08 us
  transfers between devices with their start and end apart: 69, of which 5 were waited for; matrix products, arithmetic and copies ran while one was open for 10% of the time, Pallas kernels for 0%

commit v1 on v0

v1 whole, which is shorter than its diff:
```python
import math

import jax
import jax.numpy as jnp
from jax import lax
from jax.experimental import pallas as pl
from jax.experimental.pallas import tpu as pltpu
from jax.sharding import PartitionSpec as P

DEGREE = 32
POT_LEVELS = 16
NQ = 4
ROWS = 32
NV = 16
NS = 16
NVEC = NQ * NV
PIECE = ROWS // NV
SUB = 8
CHUNKS = PIECE * SUB
HALO = CHUNKS + SUB
FIELD = (2 * ROWS + ROWS + 1) * SUB
OWN = ROWS * SUB
SITES = NS * ROWS * 1024

grid_unit = 0.0625
disorder = 2.0
F32 = jnp.float32
BF16 = jnp.bfloat16


def filter_terms(bounds):
    edges = bounds.astype(F32) * grid_unit
    center = (edges[0] + edges[1]) * 0.5
    spread = (edges[1] - edges[0]) * 0.5
    theta_lo = jnp.arccos((edges[2] - center) / spread)
    theta_hi = jnp.arccos((edges[3] - center) / spread)
    orders = jnp.arange(1, DEGREE + 1).astype(F32)
    others = 2.0 * (jnp.sin(orders * theta_lo) - jnp.sin(orders * theta_hi)) / (orders * math.pi)
    first = jnp.reshape((theta_lo - theta_hi) / math.pi, (1,))
    return jnp.concatenate([first, others, jnp.stack([2.0 / spread, center])])


def remote(src, dst, send, recv, **where):
    return pltpu.make_async_remote_copy(
        src_ref=src, dst_ref=dst, send_sem=send, recv_sem=recv,
        device_id=where, device_id_type=pl.DeviceIdType.MESH,
    )


def wait_bytes(ref, sem):
    pltpu.make_async_copy(ref, ref, sem).wait()


def split(value):
    high = value.astype(BF16)
    return high, (value - high.astype(F32)).astype(BF16)


def kernel(
    co, x_ref, pot_ref, out_ref, ritz_ref,
    even, odd, filt, diag, pot_own, slab, ops, gm, scattered, summed, total, ortho, fields,
    pot_send, pot_recv, ghost_send, ghost_recv, vec_send, vec_recv, small_send, small_recv, back_send, back_recv,
):
    s = lax.axis_index("strip")
    v = lax.axis_index("vec")

    barrier = pltpu.get_barrier_semaphore()

    def greet(j, carry):
        pl.semaphore_signal(barrier, inc=1, device_id={"vec": lax.rem(v + j, NV)}, device_id_type=pl.DeviceIdType.MESH)
        pl.semaphore_signal(barrier, inc=1, device_id={"strip": lax.rem(s + j, NS)}, device_id_type=pl.DeviceIdType.MESH)
        return carry

    lax.fori_loop(1, NV, greet, 0)

    scale = co[33]
    center = co[34]
    for r in range(ROWS // 8):
        for t in range(SUB):
            level = pot_ref[8 * r:8 * r + 8, 128 * t:128 * t + 128].astype(F32)
            field = disorder * (level / (POT_LEVELS - 1) - 0.5)
            pot_own[pl.ds(64 * r + t, 8, stride=8), :] = field
            diag[pl.ds(OWN + 64 * r + t, 8, stride=8), :] = (field - center) * scale

    for q in range(NQ):
        for r in range(ROWS // 8):
            for t in range(SUB):
                tile = x_ref[q, 8 * r:8 * r + 8, 128 * t:128 * t + 128]
                even[q, pl.ds(OWN + 64 * r + t, 8, stride=8), :] = 0.5 * tile

    pl.semaphore_wait(barrier, NV + NS - 2)

    up = lax.rem(s + NS - 1, NS)
    down = lax.rem(s + 1, NS)
    up2 = lax.rem(s + NS - 2, NS)

    def pot_copies():
        mine = diag.at[pl.ds(OWN, OWN)]
        return (
            remote(mine, diag.at[pl.ds(2 * OWN, OWN)], pot_send.at[0], pot_recv.at[0], strip=up),
            remote(mine, diag.at[pl.ds(0, OWN)], pot_send.at[1], pot_recv.at[1], strip=down),
        )

    def ghost_copies(q):
        mine = even.at[q, pl.ds(OWN, OWN)]
        return (
            remote(mine, even.at[q, pl.ds(2 * OWN, OWN)], ghost_send.at[q, 0], ghost_recv.at[q, 0], strip=up),
            remote(mine, even.at[q, pl.ds(0, OWN)], ghost_send.at[q, 1], ghost_recv.at[q, 1], strip=down),
            remote(
                even.at[q, pl.ds(OWN, SUB)], even.at[q, pl.ds(3 * OWN, SUB)],
                ghost_send.at[q, 2], ghost_recv.at[q, 2], strip=up2,
            ),
        )

    for copy in pot_copies():
        copy.start()

    def start_ghosts(q, carry):
        for copy in ghost_copies(q):
            copy.start()
        return carry

    lax.fori_loop(0, NQ, start_ghosts, 0)

    lane = lax.broadcasted_iota(jnp.int32, (1, 8, 128), 2)
    first_lane = lane == 0
    last_lane = lane == 127

    def update(q, step, low, high, double, c_now, c_next, accumulate):
        now, then = ((even, odd), (odd, even))[step]
        rows = high - low
        shape = (rows, 8, 128)
        above = now[q, (low - 1) * 8:(high - 1) * 8].reshape(shape)
        mid = now[q, low * 8:high * 8].reshape(shape)
        below = now[q, (low + 1) * 8:(high + 1) * 8].reshape(shape)
        ahead = pltpu.roll(mid, 1, 2)
        behind = pltpu.roll(mid, 127, 2)
        beside = jnp.where(first_lane, pltpu.roll(ahead, 1, 1), ahead) + jnp.where(
            last_lane, pltpu.roll(behind, 7, 1), behind
        )
        before = then[q, low * 8:high * 8].reshape(shape)
        if step == 1:
            before = before * double
        after = (diag[low * 8:high * 8].reshape(shape) * mid - before) - scale * ((above + below) + beside)
        then[q, low * 8:high * 8] = after.reshape(rows * 8, 128)
        if accumulate:
            place = slice((low - ROWS) * 8, (high - ROWS) * 8)
            term = (c_now * mid + c_next * after).reshape(rows * 8, 128)
            filt[q, place] = filt[q, place] + term

    def vec_copy(q, j):
        peer = lax.rem(v + j, NV)
        return remote(
            filt.at[q, pl.ds(peer * CHUNKS, HALO)], slab.at[pl.ds((v * NQ + q) * HALO, HALO)],
            vec_send.at[q], vec_recv.at[q], vec=peer,
        )

    for copy in pot_copies():
        copy.wait()

    def one_vector(q, carry):
        for copy in ghost_copies(q):
            copy.wait()
        odd[q] = jnp.zeros((FIELD, 128), F32)
        filt[q] = (2.0 * co[0]) * even[q, OWN:2 * OWN + SUB]
        for block in range(4):
            low, high = 8 * block + 1, 96 - 8 * block

            def pair(i, inner, block=block, low=low, high=high):
                k = 8 * block + 2 * i + 1
                double = jnp.where(k == 1, 2.0, 1.0).astype(F32)
                for step in range(2):
                    update(q, step, low, ROWS, double, 0.0, 0.0, False)
                    update(q, step, ROWS, 2 * ROWS + 1, double, co[k], co[k + 1], step == 1)
                    update(q, step, 2 * ROWS + 1, high, double, 0.0, 0.0, False)
                return inner

            lax.fori_loop(0, 4, pair, 0)
        slab[pl.ds((v * NQ + q) * HALO, HALO)] = filt[q, pl.ds(v * CHUNKS, HALO)]

        def send(j, inner):
            vec_copy(q, j).start()
            return inner

        lax.fori_loop(1, NV, send, 0)
        return carry

    lax.fori_loop(0, NQ, one_vector, 0)
    for q in range(NQ):
        wait_bytes(slab.at[pl.ds(0, (NV - 1) * HALO)], vec_recv.at[q])

    lane2 = lax.broadcasted_iota(jnp.int32, (16, 128), 1)
    pot_slab = pot_own[pl.ds(v * CHUNKS, CHUNKS)] * 0.5

    for g in range(NVEC // 16):
        def chunk(n, g=g):
            base = 16 * g * HALO + n
            return jnp.concatenate(
                [slab[pl.ds(base, 8, stride=HALO), :], slab[pl.ds(base + 8 * HALO, 8, stride=HALO), :]], axis=0
            )

        y = [chunk(n) for n in range(HALO)]
        turned = [pltpu.roll(y[n], 127, 1) for n in range(CHUNKS)]
        for n in range(CHUNKS):
            follow = n // SUB * SUB + (n + 1) % SUB
            right = jnp.where(lane2 == 127, turned[follow], turned[n])
            z = pot_slab[n:n + 1] * y[n] - (right + y[n + SUB])
            for part, value in enumerate(split(y[n]) + split(z)):
                ops[64 * part + 16 * g:64 * part + 16 * g + 16, 128 * n:128 * n + 128] = value
    prod = lax.dot_general(
        ops[...], ops[0:128, :], (((1,), (1,)), ((), ())), preferred_element_type=F32
    )
    gm[0:64] = prod[0:64] + prod[64:128]
    gm[64:128] = prod[128:192] + prod[192:256]

    def to_all(stage, count, axis, me, source, target):
        def send(j, carry):
            peer = lax.rem(me + j, count)
            remote(source(peer), target, small_send.at[stage], small_recv.at[stage], **{axis: peer}).start()
            return carry

        lax.fori_loop(1, count, send, 0)

    mine_v = pl.ds(v * 8, 8)
    mine_s = pl.ds(s * 8, 8)
    scattered[mine_v] = gm[mine_v]
    to_all(0, NV, "vec", v, lambda peer: gm.at[pl.ds(peer * 8, 8)], scattered.at[mine_v])
    wait_bytes(scattered.at[pl.ds(0, 8 * (NV - 1))], small_recv.at[0])
    summed[mine_s] = jnp.sum(scattered[...].reshape(NV, 8, 128), axis=0)
    to_all(1, NS, "strip", s, lambda peer: summed.at[mine_s], summed.at[mine_s])
    wait_bytes(summed.at[pl.ds(0, 8 * (NS - 1))], small_recv.at[1])
    total[mine_v] = jnp.sum(summed[...].reshape(NS, 8, 128), axis=0)
    to_all(2, NV, "vec", v, lambda peer: total.at[mine_v], total.at[mine_v])
    wait_bytes(total.at[pl.ds(0, 8 * (NV - 1))], small_recv.at[2])

    rows64 = lax.broadcasted_iota(jnp.int32, (64, 128), 0)
    lanes64 = lax.broadcasted_iota(jnp.int32, (64, 128), 1)
    gram = total[0:64]
    gram = gram + pltpu.roll(gram, 64, 1)
    aug = jnp.where(lanes64 < 64, gram, jnp.where(lanes64 - 64 == rows64, 1.0, 0.0))
    for k in range(NVEC):
        column = aug[:, k:k + 1] / aug[k:k + 1, k:k + 1]
        factor = jnp.where(rows64 > k, jnp.broadcast_to(column, (64, 128)), 0.0)
        aug = aug - factor * aug[k:k + 1, :]
    pivots = jnp.sum(jnp.where(rows64 == lanes64, aug, 0.0), axis=1, keepdims=True)
    inverse = (pltpu.roll(aug, 64, 1) * lax.rsqrt(pivots))[:, 0:64]

    high, low = split(math.sqrt(SITES) * inverse)
    left = jnp.concatenate(
        [jnp.concatenate([high, high], axis=1), jnp.concatenate([low, low], axis=1)], axis=0
    )
    product = jnp.dot(left, ops[0:128, :], preferred_element_type=F32)
    for n in range(CHUNKS):
        value = product[0:64, 128 * n:128 * n + 128] + product[64:128, 128 * n:128 * n + 128]
        for g in range(8):
            ortho[pl.ds(n + 8 * g * CHUNKS, 8, stride=CHUNKS), :] = value[8 * g:8 * g + 8]

    def back_copy(j, q):
        peer = lax.rem(v + j, NV)
        return remote(
            ortho.at[pl.ds((peer * NQ + q) * CHUNKS, CHUNKS)], fields.at[q, pl.ds(v * CHUNKS, CHUNKS)],
            back_send.at[0], back_recv.at[0], vec=peer,
        )

    def send_back(j, carry):
        for q in range(NQ):
            back_copy(j, q).start()
        return carry

    lax.fori_loop(1, NV, send_back, 0)
    for q in range(NQ):
        fields[q, pl.ds(v * CHUNKS, CHUNKS)] = ortho[pl.ds((v * NQ + q) * CHUNKS, CHUNKS)]

    cross = total[64:128, 0:64] + total[64:128, 64:128]
    cross = cross + cross.T
    half = jnp.dot(inverse, cross, precision=lax.Precision.HIGHEST, preferred_element_type=F32)
    ritz_ref[...] = float(ROWS) * lax.dot_general(
        inverse, half, (((1,), (1,)), ((), ())), precision=lax.Precision.HIGHEST, preferred_element_type=F32
    )

    wait_bytes(ortho.at[pl.ds(0, (NV - 1) * NQ * CHUNKS)], back_recv.at[0])
    for q in range(NQ):
        for r in range(ROWS // 8):
            for t in range(SUB):
                out_ref[q, 8 * r:8 * r + 8, 128 * t:128 * t + 128] = fields[q, pl.ds(64 * r + t, 8, stride=8), :]

    wait_bytes(ortho.at[pl.ds(0, (NV - 1) * NQ * CHUNKS)], back_send.at[0])
    for stage in range(3):
        wait_bytes(total.at[pl.ds(0, 8 * (NV - 1))], small_send.at[stage])
    for q in range(NQ):
        wait_bytes(slab.at[pl.ds(0, (NV - 1) * HALO)], vec_send.at[q])


def shards(start_vectors, potential, bounds):
    terms = filter_terms(bounds)
    vmem = pl.BlockSpec(memory_space=pltpu.VMEM)
    dma = pltpu.SemaphoreType.DMA
    return pl.pallas_call(
        kernel,
        out_shape=(
            jax.ShapeDtypeStruct((NQ, ROWS, 1024), F32),
            jax.ShapeDtypeStruct((NVEC, NVEC), F32),
        ),
        in_specs=[pl.BlockSpec(memory_space=pltpu.SMEM), vmem, vmem],
        out_specs=(vmem, vmem),
        scratch_shapes=[
            pltpu.VMEM((NQ, FIELD, 128), F32),
            pltpu.VMEM((NQ, FIELD, 128), F32),
            pltpu.VMEM((NQ, OWN + SUB, 128), F32),
            pltpu.VMEM((FIELD, 128), F32),
            pltpu.VMEM((OWN, 128), F32),
            pltpu.VMEM((NVEC * HALO, 128), F32),
            pltpu.VMEM((256, CHUNKS * 128), BF16),
            pltpu.VMEM((128, 128), F32),
            pltpu.VMEM((128, 128), F32),
            pltpu.VMEM((128, 128), F32),
            pltpu.VMEM((128, 128), F32),
            pltpu.VMEM((NVEC * CHUNKS, 128), F32),
            pltpu.VMEM((NQ, OWN, 128), F32),
            dma((2,)), dma((2,)), dma((NQ, 3)), dma((NQ, 3)), dma((NQ,)), dma((NQ,)),
            dma((3,)), dma((3,)), dma((1,)), dma((1,)),
        ],
        compiler_params=pltpu.CompilerParams(
            collective_id=0, has_side_effects=True, vmem_limit_bytes=40 << 20
        ),
        name="filter_ritz",
    )(terms, start_vectors, potential)


def solution(mesh):
    in_specs = (P("vec", "strip", None), P("strip", None), P())
    out_specs = (P("vec", "strip", None), P())
    return jax.shard_map(shards, mesh=mesh, in_specs=in_specs, out_specs=out_specs, check_vma=False)
```

time: 384 us -> 104 us (0.27)
  starting transfers between devices: 170 us -> 0 us
  Pallas kernels: 0 us -> 93.7 us
  blocking collectives: 82.5 us -> 0 us
  other arithmetic: 50.9 us -> 0.8 us
  local copies, waits for them, and re-layouts: 42 us -> 3.98 us
  waiting for transfers between devices: 27.7 us -> 0 us
    ppermute x66 -> x0, starting transfers between devices: 146 us -> none  [the longest x33 141 us: extended(): after = lax.ppermute(leading, axis, down)]
    pallas_call x0 -> x1, Pallas kernels: none -> 93.7 us  [shards(): pl.pallas_call(kernel, out_shape=(jax.ShapeDtypeStruct((NQ, ROWS, 1024),...]
    psum x1 -> x0, blocking collectives: 82.5 us -> none  [shards(): gram_sum, cross_sum = lax.psum((gram_part, cross_part), ('strip', 'vec'))]
    add x32 -> x0, other arithmetic: 35.1 us -> none  [advance(): return (current, after, filtered + coeffs[counter + 1] * after)]
    all_to_all x3 -> x0, waiting for transfers between devices: 24.8 us -> none  [the longest x1 14 us: shards(): lax.all_to_all(ortho_slab, 'vec', split_axis=0, concat_axis=1, tiled=True)]
    all_to_all x3 -> x0, starting transfers between devices: 23.9 us -> none  [the longest x1 9.64 us: shards(): lax.all_to_all(applied, 'vec', split_axis=1, concat_axis=0, tiled=True)]
    dynamic_slice x32 -> x0, local copies, waits for them, and re-layouts: 19.9 us -> none  [advance(): return (current, after, filtered + coeffs[counter + 1] * after)]
    slice x100 -> x1, local copies, waits for them, and re-layouts: 13.9 us -> 0.62 us  [filter_terms(): theta_lo = jnp.arccos((edges[2] - center) / spread)]
  transfers between devices with their start and end apart: 69 -> 0, of which waited for: 5 -> 0; matrix products, arithmetic and copies ran while one was open for 10% -> 0% of each run, Pallas kernels for 0% -> 0%
where the time goes in v1:
time: 104 us; the launch traced here: 103 us
  Pallas kernels  93.7 us (90%)
  between operations  4.74 us (5%)
  local copies, waits for them, and re-layouts  3.98 us (4%)
    pallas_call x1, Pallas kernels, shards(): pl.pallas_call(kernel, out_shape=(jax.ShapeDtypeStruct((NQ, ROWS, 1024),...  93.7 us
    unnamed x6, local copies, waits for them, and re-layouts  3.36 us

profile of v1, /device:TPU:1, one launch (start us, length us, event | category | flops | bytes accessed | tf_op | source)
XLA Modules:
  0.0 103.2 jit_solution(18300107739583248518)
XLA Ops:
  0.6 0.7 convert_multiply_fusion
  1.3 0.6 fusion
  6.0 0.1 multiply_divide_fusion
  6.1 0.1 pad_maximum_fusion.co
  6.1 0.0 copy-start
  6.2 1.0 %copy-done = f32[4,32,1024]{2,1,0:T(8,128)S(1)} copy-done((f32[4,32,1024]{2,1,0:T(8,128)S(1)}, f32[4,32,1024]{2,1,0:T(8,128)}, u32[]{:S(2)}) %copy-start) | copy-done | bytes 524312
  7.2 0.0 copy-start.1
  7.2 0.9 copy-done.1
  8.1 93.7 %filter_ritz.1 = (f32[4,32,1024]{2,1,0:T(8,128)S(1)}, f32[64,64]{1,0:T(8,128)S(1)}) custom-call(f32[35]{0:T(128)S(1)} %pad_maximum_fusion.co, f32[4,32,1024]{2,1,0:T(8,128)S(1)} %copy-done, s32[32,1024]{1,0:T(8,128)S(1)} %copy-done.1), custom_call_target="tpu_custom_call" | custom-call | tf_op jit(solution)/shard_map/filter_ritz/pallas_call | solution.py:298
  101.8 0.8 copy.7
  102.6 0.6 copy.8
Async XLA Ops:
  6.1 1.0 %copy-start = (f32[4,32,1024]{2,1,0:T(8,128)S(1)}, f32[4,32,1024]{2,1,0:T(8,128)}, u32[]{:S(2)}) copy-start(f32[4,32,1024]{2,1,0:T(8,128)} %x_ref.1) | copy-start | bytes 1572868
  7.2 0.9 copy-start.1

commit v2 on v1

v2 whole, which is shorter than its diff:
```python
import math

import jax
import jax.numpy as jnp
from jax import lax
from jax.experimental import pallas as pl
from jax.experimental.pallas import tpu as pltpu
from jax.sharding import PartitionSpec as P

DEGREE = 32
POT_LEVELS = 16
NQ = 4
ROWS = 32
NV = 16
NS = 16
NVEC = NQ * NV
PIECE = ROWS // NV
SUB = 8
CHUNKS = PIECE * SUB
HALO = CHUNKS + SUB
FIELD = (3 * ROWS + 1) * SUB
PAIRS = 3 * ROWS // 2 + 1
NA = 8
NB = 32
OWN = ROWS * SUB
HALF_PI = math.pi / 2
SITES = NS * ROWS * 1024

grid_unit = 0.0625
disorder = 2.0
F32 = jnp.float32
BF16 = jnp.bfloat16


def remote(src, dst, send, recv, **where):
    return pltpu.make_async_remote_copy(
        src_ref=src, dst_ref=dst, send_sem=send, recv_sem=recv,
        device_id=where, device_id_type=pl.DeviceIdType.MESH,
    )


def wait_bytes(ref, sem):
    pltpu.make_async_copy(ref, ref, sem).wait()


def split(value):
    high = value.astype(BF16)
    return high, (value - high.astype(F32)).astype(BF16)


def arccos(x):
    size = jnp.abs(x)
    large = size > 0.5
    square = jnp.where(large, 0.5 * (1.0 - size), x * x)
    base = jnp.where(large, jnp.sqrt(square), size)
    poly = 4.2163199048e-2 * square + 2.4181311049e-2
    poly = poly * square + 4.5470025998e-2
    poly = poly * square + 7.4953002686e-2
    poly = poly * square + 1.6666752422e-1
    arcsin = base + base * square * poly
    positive = jnp.where(large, 2.0 * arcsin, HALF_PI - arcsin)
    return jnp.where(x < 0.0, math.pi - positive, positive)


def place(s):
    return 4 * (s % 2) + s // 2


def turn_blocks(tiles):
    tiles = list(tiles)
    block = lax.broadcasted_iota(jnp.int32, tiles[0].shape, 1) // 16
    for bit in (1, 2, 4):
        clear = (block & bit) == 0
        for i in range(8):
            if i & bit == 0:
                one, two = tiles[i], tiles[i + bit]
                tiles[i] = jnp.where(clear, one, pltpu.roll(two, 16 * bit, 1))
                tiles[i + bit] = jnp.where(clear, pltpu.roll(one, 128 - 16 * bit, 1), two)
    return tiles


def to_classes(tiles):
    lane = lax.broadcasted_iota(jnp.int32, tiles[0].shape, 1)
    index = 8 * (lane % 16) + lane // 16
    return turn_blocks([jnp.take_along_axis(tile, index, axis=1) for tile in tiles])


def from_classes(tiles):
    lane = lax.broadcasted_iota(jnp.int32, tiles[0].shape, 1)
    index = 16 * (lane % 8) + lane // 8
    return [jnp.take_along_axis(tile, index, axis=1) for tile in turn_blocks(tiles)]


def kernel(
    bounds_ref, x_hbm, pot_hbm, out_ref, ritz_ref,
    x_ref, pot_ref, coef, start, even, odd, filt, filtered, diag_rows, diag, pot_own, slab, ops, apply_ops,
    gm, scattered, summed, total, ortho, fields,
    in_sem, pot_send, pot_recv, ghost_send, ghost_recv, vec_send, vec_recv, small_send, small_recv,
    back_send, back_recv,
):
    s = lax.axis_index("strip")
    v = lax.axis_index("vec")
    y_lo = s // 2 % 2
    along = s // 4 * 2 + s % 2
    across = y_lo * NV + v
    flipped = s + 2 - 4 * y_lo

    barrier = pltpu.get_barrier_semaphore()

    def greet(j, carry):
        peer = lax.rem(v + j, NV)
        for where in ({"strip": s, "vec": peer}, {"strip": flipped, "vec": peer}, {"strip": lax.rem(s + j, NS), "vec": v}):
            pl.semaphore_signal(barrier, inc=1, device_id=where, device_id_type=pl.DeviceIdType.MESH)
        return carry

    pot_in = pltpu.make_async_copy(pot_hbm, pot_ref, in_sem.at[0])
    x_in = pltpu.make_async_copy(x_hbm, x_ref, in_sem.at[1])
    pot_in.start()
    x_in.start()
    lax.fori_loop(1, NV, greet, 0)

    def splat(i):
        return jnp.full((8, 128), bounds_ref[i], jnp.int32).astype(F32) * grid_unit

    edges = [splat(i) for i in range(4)]
    center = (edges[0] + edges[1]) * 0.5
    spread = (edges[1] - edges[0]) * 0.5
    scale = 2.0 / spread

    pot_in.wait()
    for r in range(ROWS // 8):
        tiles = []
        for t in range(SUB):
            level = pot_ref[8 * r:8 * r + 8, 128 * t:128 * t + 128].astype(F32)
            tiles.append(disorder * (level / (POT_LEVELS - 1) - 0.5))
        for c, field in enumerate(to_classes(tiles)):
            pot_own[pl.ds(64 * r + place(c), 8, stride=8), :] = field
            diag_rows[pl.ds(OWN + 64 * r + place(c), 8, stride=8), :] = (field - center) * scale

    x_in.wait()

    def classes_of(q, carry):
        for r in range(ROWS // 8):
            tiles = [0.5 * x_ref[q, 8 * r:8 * r + 8, 128 * t:128 * t + 128] for t in range(SUB)]
            for c, tile in enumerate(to_classes(tiles)):
                start[q, pl.ds(OWN + 64 * r + place(c), 8, stride=8), :] = tile
        return carry

    lax.fori_loop(0, NQ, classes_of, 0)

    pl.semaphore_wait(barrier, 3 * (NV - 1))

    up = lax.rem(s + NS - 1, NS)
    down = lax.rem(s + 1, NS)
    up2 = lax.rem(s + NS - 2, NS)

    def pot_copies():
        mine = diag_rows.at[pl.ds(OWN, OWN)]
        return (
            remote(mine, diag_rows.at[pl.ds(2 * OWN, OWN)], pot_send.at[0], pot_recv.at[0], strip=up),
            remote(mine, diag_rows.at[pl.ds(0, OWN)], pot_send.at[1], pot_recv.at[1], strip=down),
        )

    def ghost_copies(q):
        mine = start.at[q, pl.ds(OWN, OWN)]
        return (
            remote(mine, start.at[q, pl.ds(2 * OWN, OWN)], ghost_send.at[q, 0], ghost_recv.at[q, 0], strip=up),
            remote(mine, start.at[q, pl.ds(0, OWN)], ghost_send.at[q, 1], ghost_recv.at[q, 1], strip=down),
            remote(
                start.at[q, pl.ds(OWN, SUB)], start.at[q, pl.ds(3 * OWN, SUB)],
                ghost_send.at[q, 2], ghost_recv.at[q, 2], strip=up2,
            ),
        )

    def start_ghosts(q):
        for copy in ghost_copies(q):
            copy.start()

    for copy in pot_copies():
        copy.start()
    start_ghosts(0)

    theta_lo = arccos((edges[2] - center) / spread)
    theta_hi = arccos((edges[3] - center) / spread)
    coef[0:8] = (theta_lo - theta_hi) / math.pi

    def coefficient(k, carry):
        order = jnp.full((8, 128), k, jnp.int32).astype(F32)
        coef[pl.ds(pl.multiple_of(8 * k, 8), 8)] = (
            2.0 * (jnp.sin(order * theta_lo) - jnp.sin(order * theta_hi)) / (order * math.pi)
        )
        return carry

    lax.fori_loop(1, DEGREE + 1, coefficient, 0)

    def pair_place(row):
        return (16 * row, 0) if row <= 48 else (16 * (96 - row), 1)

    for copy in pot_copies():
        copy.wait()
    for row in range(1, 3 * ROWS):
        value = diag_rows[8 * row:8 * row + 8]
        for base, half in {pair_place(row), (16 * (96 - row), 1) if row == 48 else pair_place(row)}:
            diag[pl.ds(base + half, 8, stride=2), :] = value

    sub = lax.broadcasted_iota(jnp.int32, (8, 128), 0)
    lane = lax.broadcasted_iota(jnp.int32, (8, 128), 1)
    index_left = jnp.where(sub >= 6, (lane + 127) % 128, lane)
    index_right = jnp.where(sub < 2, (lane + 1) % 128, lane)
    upper = (sub % 2 == 0)[None, None]

    def update(step, low, high, double, c_now, c_next, accumulate):
        now, then = ((even, odd), (odd, even))[step]
        rows = high - low
        flat = (rows, 8, 128)
        top = min(high + 1, PAIRS)
        ext = now[(low - 1) * 16:top * 16].reshape(top - low + 1, 2, 8, 128)
        above = ext[0:rows]
        mid = ext[1:rows + 1]
        if high == PAIRS:
            crossing = ext[rows - 1:rows]
            crossing = jnp.where(upper, pltpu.roll(crossing, 7, 2), pltpu.roll(crossing, 1, 2))
            below = jnp.concatenate([ext[2:rows + 1], crossing], axis=0)
        else:
            below = ext[2:rows + 2]
        left = pltpu.roll(jnp.take_along_axis(mid[:, 1], jnp.broadcast_to(index_left[None], flat), axis=2), 2, 1)
        right = pltpu.roll(jnp.take_along_axis(mid[:, 0], jnp.broadcast_to(index_right[None], flat), axis=2), 6, 1)
        before = then[low * 16:high * 16].reshape(rows, 2, 8, 128)
        local = diag[low * 16:high * 16].reshape(rows, 2, 8, 128)
        parts = []
        for j, beside in enumerate((left + mid[:, 1], mid[:, 0] + right)):
            old = before[:, j]
            if step == 1:
                old = old * double
            parts.append((local[:, j] * mid[:, j] - old) - scale * ((above[:, j] + below[:, j]) + beside))
        after = jnp.stack(parts, axis=1)
        then[low * 16:high * 16] = after.reshape(rows * 16, 128)
        if accumulate:
            term = (c_now * mid + c_next * after).reshape(rows * 16, 128)
            filt[...] = filt[...] + term

    def vec_copy(q, j):
        peer = lax.rem(v + j, NV)
        return remote(
            filtered.at[q, pl.ds(peer * CHUNKS, HALO)], slab.at[pl.ds((v * NQ + q) * HALO, HALO)],
            vec_send.at[q], vec_recv.at[q], vec=peer,
        )

    def one_vector(q, carry):
        for copy in ghost_copies(q):
            copy.wait()

        @pl.when(q < NQ - 1)
        def _():
            start_ghosts(q + 1)

        for row in range(3 * ROWS + 1):
            value = start[q, 8 * row:8 * row + 8]
            base, half = pair_place(row)
            even[pl.ds(base + half, 8, stride=2), :] = value
            if row == 48:
                even[pl.ds(base + 1, 8, stride=2), :] = value
        odd[...] = jnp.zeros((16 * PAIRS, 128), F32)
        filt[...] = (
            (2.0 * coef[0:8]) * even[16 * ROWS:16 * PAIRS].reshape(2 * (PAIRS - ROWS), 8, 128)
        ).reshape(16 * (PAIRS - ROWS), 128)
        for block in range(4):
            low = 8 * block + 1

            def pair(i, inner, block=block, low=low):
                k = 8 * block + 2 * i + 1
                double = jnp.where(k == 1, 2.0, 1.0).astype(F32)
                c_now = coef[pl.ds(pl.multiple_of(8 * k, 8), 8)]
                c_next = coef[pl.ds(pl.multiple_of(8 * k + 8, 8), 8)]
                for step in range(2):
                    update(step, low, ROWS, double, None, None, False)
                    update(step, ROWS, PAIRS, double, c_now, c_next, step == 1)
                return inner

            lax.fori_loop(0, 4, pair, 0)
        for row in range(ROWS + 1):
            base, half = pair_place(ROWS + row)
            filtered[q, 8 * row:8 * row + 8] = filt[pl.ds(base - 16 * ROWS + half, 8, stride=2), :]
        slab[pl.ds((v * NQ + q) * HALO, HALO)] = filtered[q, pl.ds(v * CHUNKS, HALO)]

        def send(j, inner):
            vec_copy(q, j).start()
            return inner

        lax.fori_loop(1, NV, send, 0)
        return carry

    lax.fori_loop(0, NQ, one_vector, 0)
    for q in range(NQ):
        wait_bytes(slab.at[pl.ds(0, (NV - 1) * HALO)], vec_recv.at[q])

    lane16 = lax.broadcasted_iota(jnp.int32, (16, 128), 1)
    pot_slab = pot_own[pl.ds(v * CHUNKS, CHUNKS)] * 0.5

    def chunk(g, n):
        base = 16 * g * HALO + n
        return jnp.concatenate(
            [slab[pl.ds(base, 8, stride=HALO), :], slab[pl.ds(base + 8 * HALO, 8, stride=HALO), :]], axis=0
        )

    for g in range(NVEC // 16):
        y = [chunk(g, n) for n in range(HALO)]
        for row in range(PIECE):
            for c in range(SUB):
                n = SUB * row + place(c)
                if c < SUB - 1:
                    right = y[SUB * row + place(c + 1)]
                else:
                    right = pltpu.roll(y[SUB * row + place(0)], 127, 1)
                z = pot_slab[n:n + 1] * y[n] - (right + y[n + SUB])
                for part, value in enumerate(split(y[n]) + split(z)):
                    ops[64 * part + 16 * g:64 * part + 16 * g + 16, 128 * n:128 * n + 128] = value
    prod = lax.dot_general(
        ops[...], ops[0:128, :], (((1,), (1,)), ((), ())), preferred_element_type=F32
    )
    rows64 = lax.broadcasted_iota(jnp.int32, (64, 128), 0)
    lanes64 = lax.broadcasted_iota(jnp.int32, (64, 128), 1)
    gram_part = prod[0:64] + prod[64:128]
    cross_part = prod[128:192] + prod[192:256]
    gm[...] = jnp.where(
        lanes64 < 64, gram_part + pltpu.roll(gram_part, 64, 1), cross_part + pltpu.roll(cross_part, 64, 1)
    )

    def to_along(stage, source, target):
        def send(j, carry):
            peer = lax.rem(along + j, NA)
            strip = peer // 2 * 4 + y_lo * 2 + peer % 2
            remote(source(peer), target, small_send.at[stage], small_recv.at[stage], strip=strip).start()
            return carry

        lax.fori_loop(1, NA, send, 0)

    mine_a = pl.ds(along * 8, 8)
    mine_b = pl.ds(across * 8, 8)
    scattered[mine_a] = gm[mine_a]
    to_along(0, lambda peer: gm.at[pl.ds(peer * 8, 8)], scattered.at[mine_a])

    for g in range(NVEC // 16):
        for row in range(PIECE):
            tiles = from_classes([chunk(g, SUB * row + place(c)) for c in range(SUB)])
            for t, tile in enumerate(tiles):
                n = SUB * row + t
                for part, value in enumerate(split(tile)):
                    apply_ops[64 * part + 16 * g:64 * part + 16 * g + 16, 128 * n:128 * n + 128] = value

    wait_bytes(scattered.at[pl.ds(0, 8 * (NA - 1))], small_recv.at[0])
    summed[mine_b] = jnp.sum(scattered[...].reshape(NA, 8, 128), axis=0)

    def send_across(j, carry):
        peer = lax.rem(across + j, NB)
        strip = s + 2 * (peer // NV - y_lo)
        remote(
            summed.at[mine_b], summed.at[mine_b], small_send.at[1], small_recv.at[1], strip=strip, vec=peer % NV
        ).start()
        return carry

    lax.fori_loop(1, NB, send_across, 0)
    wait_bytes(summed.at[pl.ds(0, 8 * (NB - 1))], small_recv.at[1])
    total[mine_a] = jnp.sum(summed[...].reshape(NB, 8, 128), axis=0)
    to_along(2, lambda peer: total.at[mine_a], total.at[mine_a])
    wait_bytes(total.at[pl.ds(0, 8 * (NA - 1))], small_recv.at[2])

    aug = jnp.where(lanes64 < 64, total[...], jnp.where(lanes64 - 64 == rows64, 1.0, 0.0))
    for k in range(NVEC):
        column = aug[:, k:k + 1] / aug[k:k + 1, k:k + 1]
        factor = jnp.where(rows64 > k, jnp.broadcast_to(column, (64, 128)), 0.0)
        aug = aug - factor * aug[k:k + 1, :]
    pivots = jnp.sum(jnp.where(rows64 == lanes64, aug, 0.0), axis=1, keepdims=True)
    inverse = (pltpu.roll(aug, 64, 1) * lax.rsqrt(pivots))[:, 0:64]

    high, low = split(math.sqrt(SITES) * inverse)
    left = jnp.concatenate(
        [jnp.concatenate([high, high], axis=1), jnp.concatenate([low, low], axis=1)], axis=0
    )
    product = jnp.dot(left, apply_ops[...], preferred_element_type=F32)
    for n in range(CHUNKS):
        value = product[0:64, 128 * n:128 * n + 128] + product[64:128, 128 * n:128 * n + 128]
        for g in range(8):
            ortho[pl.ds(n + 8 * g * CHUNKS, 8, stride=CHUNKS), :] = value[8 * g:8 * g + 8]

    def back_copy(j, q):
        peer = lax.rem(v + j, NV)
        return remote(
            ortho.at[pl.ds((peer * NQ + q) * CHUNKS, CHUNKS)], fields.at[q, pl.ds(v * CHUNKS, CHUNKS)],
            back_send.at[0], back_recv.at[0], vec=peer,
        )

    def send_back(j, carry):
        for q in range(NQ):
            back_copy(j, q).start()
        return carry

    lax.fori_loop(1, NV, send_back, 0)
    for q in range(NQ):
        fields[q, pl.ds(v * CHUNKS, CHUNKS)] = ortho[pl.ds((v * NQ + q) * CHUNKS, CHUNKS)]

    cross = pltpu.roll(total[...], 64, 1)[:, 0:64]
    cross = cross + cross.T
    half = jnp.dot(inverse, cross, precision=lax.Precision.HIGHEST, preferred_element_type=F32)
    ritz_ref[...] = float(ROWS) * lax.dot_general(
        inverse, half, (((1,), (1,)), ((), ())), precision=lax.Precision.HIGHEST, preferred_element_type=F32
    )

    wait_bytes(ortho.at[pl.ds(0, (NV - 1) * NQ * CHUNKS)], back_recv.at[0])
    for q in range(NQ):
        for r in range(ROWS // 8):
            for t in range(SUB):
                out_ref[q, 8 * r:8 * r + 8, 128 * t:128 * t + 128] = fields[q, pl.ds(64 * r + t, 8, stride=8), :]

    wait_bytes(ortho.at[pl.ds(0, (NV - 1) * NQ * CHUNKS)], back_send.at[0])
    wait_bytes(scattered.at[pl.ds(0, 8 * (NA - 1))], small_send.at[0])
    wait_bytes(summed.at[pl.ds(0, 8 * (NB - 1))], small_send.at[1])
    wait_bytes(scattered.at[pl.ds(0, 8 * (NA - 1))], small_send.at[2])
    for q in range(NQ):
        wait_bytes(slab.at[pl.ds(0, (NV - 1) * HALO)], vec_send.at[q])


def shards(start_vectors, potential, bounds):
    vmem = pl.BlockSpec(memory_space=pltpu.VMEM)
    hbm = pl.BlockSpec(memory_space=pltpu.HBM)
    dma = pltpu.SemaphoreType.DMA
    return pl.pallas_call(
        kernel,
        out_shape=(
            jax.ShapeDtypeStruct((NQ, ROWS, 1024), F32),
            jax.ShapeDtypeStruct((NVEC, NVEC), F32),
        ),
        in_specs=[pl.BlockSpec(memory_space=pltpu.SMEM), hbm, hbm],
        out_specs=(vmem, vmem),
        scratch_shapes=[
            pltpu.VMEM((NQ, ROWS, 1024), F32),
            pltpu.VMEM((ROWS, 1024), jnp.int32),
            pltpu.VMEM((8 * (DEGREE + 1), 128), F32),
            pltpu.VMEM((NQ, FIELD, 128), F32),
            pltpu.VMEM((16 * PAIRS, 128), F32),
            pltpu.VMEM((16 * PAIRS, 128), F32),
            pltpu.VMEM((16 * (PAIRS - ROWS), 128), F32),
            pltpu.VMEM((NQ, OWN + SUB, 128), F32),
            pltpu.VMEM((FIELD, 128), F32),
            pltpu.VMEM((16 * PAIRS, 128), F32),
            pltpu.VMEM((OWN, 128), F32),
            pltpu.VMEM((NVEC * HALO, 128), F32),
            pltpu.VMEM((256, CHUNKS * 128), BF16),
            pltpu.VMEM((128, CHUNKS * 128), BF16),
            pltpu.VMEM((64, 128), F32),
            pltpu.VMEM((8 * NA, 128), F32),
            pltpu.VMEM((8 * NB, 128), F32),
            pltpu.VMEM((64, 128), F32),
            pltpu.VMEM((NVEC * CHUNKS, 128), F32),
            pltpu.VMEM((NQ, OWN, 128), F32),
            dma((2,)), dma((2,)), dma((2,)), dma((NQ, 3)), dma((NQ, 3)), dma((NQ,)), dma((NQ,)),
            dma((3,)), dma((3,)), dma((1,)), dma((1,)),
        ],
        compiler_params=pltpu.CompilerParams(
            collective_id=0, has_side_effects=True, vmem_limit_bytes=40 << 20
        ),
        name="filter_ritz",
    )(bounds, start_vectors, potential)


def solution(mesh):
    in_specs = (P("vec", "strip", None), P("strip", None), P())
    out_specs = (P("vec", "strip", None), P())
    return jax.shard_map(shards, mesh=mesh, in_specs=in_specs, out_specs=out_specs, check_vma=False)
```

time: 104 us -> 90.5 us (0.87)
  Pallas kernels: 93.7 us -> 85.7 us
  between operations: 4.74 us -> 0.65 us
    pallas_call x1, Pallas kernels: 93.7 us -> 85.7 us  [shards(): pl.pallas_call(kernel, out_shape=(jax.ShapeDtypeStruct((NQ, ROWS, 1024),...]
    unnamed x6 -> x8, local copies, waits for them, and re-layouts: 3.36 us -> 4 us
where the time goes in v2:
time: 90.5 us; the launch traced here: 90.3 us
  Pallas kernels  85.7 us (95%)
  local copies, waits for them, and re-layouts  4 us (4%)
    pallas_call x1, Pallas kernels, shards(): pl.pallas_call(kernel, out_shape=(jax.ShapeDtypeStruct((NQ, ROWS, 1024),...  85.7 us
    unnamed x8, local copies, waits for them, and re-layouts  4 us

profile of v2, /device:TPU:1, one launch (start us, length us, event | category | flops | bytes accessed | tf_op | source)
XLA Modules:
  0.0 90.3 jit_solution(7653627839485055251)
XLA Ops:
  0.6 0.0 copy-start
  0.6 1.0 %copy-done = f32[4,32,1024]{2,1,0:T(8,128)S(1)} copy-done((f32[4,32,1024]{2,1,0:T(8,128)S(1)}, f32[4,32,1024]{2,1,0:T(8,128)}, u32[]{:S(2)}) %copy-start) | copy-done | bytes 524312
  1.7 0.0 copy-start.1
  1.7 0.9 copy-done.1
  2.6 0.0 copy-start.2
  2.6 0.7 copy-done.2
  3.2 85.7 %filter_ritz.1 = (f32[4,32,1024]{2,1,0:T(8,128)S(1)}, f32[64,64]{1,0:T(8,128)S(1)}) custom-call(s32[4]{0:T(128)S(1)} %copy-done.2, f32[4,32,1024]{2,1,0:T(8,128)S(1)} %copy-done, s32[32,1024]{1,0:T(8,128)S(1)} %copy-done.1), custom_call_target="tpu_custom_call" | custom-call | tf_op jit(solution)/shard_map/filter_ritz/pallas_call | solution.py:427
  88.9 0.8 copy.7
  89.7 0.6 copy.8
Async XLA Ops:
  0.6 1.0 %copy-start = (f32[4,32,1024]{2,1,0:T(8,128)S(1)}, f32[4,32,1024]{2,1,0:T(8,128)}, u32[]{:S(2)}) copy-start(f32[4,32,1024]{2,1,0:T(8,128)} %x_hbm.1) | copy-start | bytes 1572868
  1.7 0.9 %copy-start.1 = (s32[32,1024]{1,0:T(8,128)S(1)}, s32[32,1024]{1,0:T(8,128)}, u32[]{:S(2)}) copy-start(s32[32,1024]{1,0:T(8,128)} %pot_hbm.1) | copy-start | bytes 393220
  2.6 0.7 copy-start.2

commit v3 on v2

--- a/solution.py
+++ b/solution.py
@@ -91,10 +91,41 @@
     return [jnp.take_along_axis(tile, index, axis=1) for tile in turn_blocks(tiles)]
 
 
+def inverse_factor(aug):
+    rows = [aug[8 * i:8 * i + 8] for i in range(8)]
+    sub = lax.broadcasted_iota(jnp.int32, (8, 128), 0)
+    done = []
+
+    def spread(value, k):
+        return jnp.broadcast_to(value[k:k + 1], (8, 128))
+
+    for p in range(8):
+        columns = {
+            (j, i): jnp.broadcast_to(rows[i][:, 8 * p + j:8 * p + j + 1], (8, 128))
+            for i in range(p, 8) for j in range(8)
+        }
+        pivots = spread(columns[0, p], 0)
+        for k in range(8):
+            pivot = spread(columns[k, p], k)
+            pivots = jnp.where(sub == k, pivot, pivots)
+            inverse = 1.0 / pivot
+            row = spread(rows[p], k)
+            heads = {j: spread(columns[j, p], k) for j in range(k + 1, 8)}
+            for i in range(p, 8):
+                factor = columns[k, i] * inverse
+                if i == p:
+                    factor = jnp.where(sub > k, factor, 0.0)
+                rows[i] = rows[i] - factor * row
+                for j in range(k + 1, 8):
+                    columns[j, i] = columns[j, i] - factor * heads[j]
+        done.append(pltpu.roll(rows[p], 64, 1) * lax.rsqrt(pivots))
+    return jnp.concatenate(done, axis=0)[:, 0:64]
+
+
 def kernel(
-    bounds_ref, x_hbm, pot_hbm, out_ref, ritz_ref,
+    bounds_ref, x_hbm, pot_hbm, fields, ritz_ref,
     x_ref, pot_ref, coef, start, even, odd, filt, filtered, diag_rows, diag, pot_own, slab, ops, apply_ops,
-    gm, scattered, summed, total, ortho, fields,
+    gm, scattered, summed, total, ortho,
     in_sem, pot_send, pot_recv, ghost_send, ghost_recv, vec_send, vec_recv, small_send, small_recv,
     back_send, back_recv,
 ):
@@ -365,13 +396,7 @@
     to_along(2, lambda peer: total.at[mine_a], total.at[mine_a])
     wait_bytes(total.at[pl.ds(0, 8 * (NA - 1))], small_recv.at[2])
 
-    aug = jnp.where(lanes64 < 64, total[...], jnp.where(lanes64 - 64 == rows64, 1.0, 0.0))
-    for k in range(NVEC):
-        column = aug[:, k:k + 1] / aug[k:k + 1, k:k + 1]
-        factor = jnp.where(rows64 > k, jnp.broadcast_to(column, (64, 128)), 0.0)
-        aug = aug - factor * aug[k:k + 1, :]
-    pivots = jnp.sum(jnp.where(rows64 == lanes64, aug, 0.0), axis=1, keepdims=True)
-    inverse = (pltpu.roll(aug, 64, 1) * lax.rsqrt(pivots))[:, 0:64]
+    inverse = inverse_factor(jnp.where(lanes64 < 64, total[...], jnp.where(lanes64 - 64 == rows64, 1.0, 0.0)))
 
     high, low = split(math.sqrt(SITES) * inverse)
     left = jnp.concatenate(
@@ -407,11 +432,6 @@
     )
 
     wait_bytes(ortho.at[pl.ds(0, (NV - 1) * NQ * CHUNKS)], back_recv.at[0])
-    for q in range(NQ):
-        for r in range(ROWS // 8):
-            for t in range(SUB):
-                out_ref[q, 8 * r:8 * r + 8, 128 * t:128 * t + 128] = fields[q, pl.ds(64 * r + t, 8, stride=8), :]
-
     wait_bytes(ortho.at[pl.ds(0, (NV - 1) * NQ * CHUNKS)], back_send.at[0])
     wait_bytes(scattered.at[pl.ds(0, 8 * (NA - 1))], small_send.at[0])
     wait_bytes(summed.at[pl.ds(0, 8 * (NB - 1))], small_send.at[1])
@@ -420,16 +440,22 @@
         wait_bytes(slab.at[pl.ds(0, (NV - 1) * HALO)], vec_send.at[q])
 
 
+def arrange(fields, ritz, out_ref, ritz_ref):
+    for q in range(NQ):
+        for r in range(ROWS // 8):
+            for t in range(SUB):
+                out_ref[q, 8 * r:8 * r + 8, 128 * t:128 * t + 128] = fields[q, pl.ds(64 * r + t, 8, stride=8), :]
+    ritz_ref[...] = ritz[...]
+
+
 def shards(start_vectors, potential, bounds):
     vmem = pl.BlockSpec(memory_space=pltpu.VMEM)
     hbm = pl.BlockSpec(memory_space=pltpu.HBM)
     dma = pltpu.SemaphoreType.DMA
-    return pl.pallas_call(
+    ritz_shape = jax.ShapeDtypeStruct((NVEC, NVEC), F32)
+    fields, ritz = pl.pallas_call(
         kernel,
-        out_shape=(
-            jax.ShapeDtypeStruct((NQ, ROWS, 1024), F32),
-            jax.ShapeDtypeStruct((NVEC, NVEC), F32),
-        ),
+        out_shape=(jax.ShapeDtypeStruct((NQ, OWN, 128), F32), ritz_shape),
         in_specs=[pl.BlockSpec(memory_space=pltpu.SMEM), hbm, hbm],
         out_specs=(vmem, vmem),
         scratch_shapes=[
@@ -452,15 +478,21 @@
             pltpu.VMEM((8 * NB, 128), F32),
             pltpu.VMEM((64, 128), F32),
             pltpu.VMEM((NVEC * CHUNKS, 128), F32),
-            pltpu.VMEM((NQ, OWN, 128), F32),
             dma((2,)), dma((2,)), dma((2,)), dma((NQ, 3)), dma((NQ, 3)), dma((NQ,)), dma((NQ,)),
             dma((3,)), dma((3,)), dma((1,)), dma((1,)),
         ],
         compiler_params=pltpu.CompilerParams(
-            collective_id=0, has_side_effects=True, vmem_limit_bytes=40 << 20
+            collective_id=0, has_side_effects=True, vmem_limit_bytes=63 << 20
         ),
         name="filter_ritz",
     )(bounds, start_vectors, potential)
+    return pl.pallas_call(
+        arrange,
+        out_shape=(jax.ShapeDtypeStruct((NQ, ROWS, 1024), F32), ritz_shape),
+        in_specs=[vmem, vmem],
+        out_specs=(vmem, vmem),
+        name="arrange",
+    )(fields, ritz)
 
 
 def solution(mesh):

time: 90.5 us -> 85.5 us (0.945)
  local copies, waits for them, and re-layouts: 4 us -> 0 us
  Pallas kernels: 85.7 us -> 84.7 us
    unnamed x8 -> x0, local copies, waits for them, and re-layouts: 4 us -> none
    pallas_call x1 -> x2, Pallas kernels: 85.7 us -> 84.7 us  [the longest x1 82.8 us: shards(): pl.pallas_call(kernel, out_shape=(jax.ShapeDtypeStruct((NQ, OWN, 128), F3...]
where the time goes in v3:
time: 85.5 us; the launch traced here: 85.3 us
  Pallas kernels  84.7 us (99%)
    pallas_call x1, Pallas kernels, shards(): pl.pallas_call(kernel, out_shape=(jax.ShapeDtypeStruct((NQ, OWN, 128), F3...  82.8 us
    pallas_call x1, Pallas kernels, shards(): pl.pallas_call(arrange, out_shape=(jax.ShapeDtypeStruct((NQ, ROWS, 1024),...  1.94 us

profile of v3, /device:TPU:1, one launch (start us, length us, event | category | flops | bytes accessed | tf_op | source)
XLA Modules:
  0.0 85.3 jit_solution(12038485318030789240)
XLA Ops:
  0.6 82.8 %filter_ritz.1 = (f32[4,256,128]{2,1,0:T(8,128)}, f32[64,64]{1,0:T(8,128)}) custom-call(s32[4]{0:T(128)} %bounds_ref.1, f32[4,32,1024]{2,1,0:T(8,128)} %x_hbm.1, s32[32,1024]{1,0:T(8,128)} %pot_hbm.1), custom_call_target="tpu_custom_call" | custom-call | tf_op jit(solution)/shard_map/filter_ritz/pallas_call | solution.py:456
  83.4 1.9 %arrange.1 = (f32[4,32,1024]{2,1,0:T(8,128)}, f32[64,64]{1,0:T(8,128)}) custom-call(f32[4,256,128]{2,1,0:T(8,128)} %get-tuple-element.4.fields, f32[64,64]{1,0:T(8,128)} %get-tuple-element.5.ritz), custom_call_target="tpu_custom_call" | custom-call | tf_op jit(solution)/shard_map/arrange/pallas_call | solution.py:489

commit v4 on v3

--- a/solution.py
+++ b/solution.py
@@ -177,7 +177,7 @@
                 start[q, pl.ds(OWN + 64 * r + place(c), 8, stride=8), :] = tile
         return carry
 
-    lax.fori_loop(0, NQ, classes_of, 0)
+    classes_of(0, 0)
 
     pl.semaphore_wait(barrier, 3 * (NV - 1))
 
@@ -210,6 +210,7 @@
     for copy in pot_copies():
         copy.start()
     start_ghosts(0)
+    lax.fori_loop(1, NQ, classes_of, 0)
 
     theta_lo = arccos((edges[2] - center) / spread)
     theta_hi = arccos((edges[3] - center) / spread)
@@ -240,10 +241,13 @@
     index_right = jnp.where(sub < 2, (lane + 1) % 128, lane)
     upper = (sub % 2 == 0)[None, None]
 
-    def update(step, low, high, double, c_now, c_next, accumulate):
-        now, then = ((even, odd), (odd, even))[step]
+    def shift(value, index, by):
+        index = jnp.broadcast_to(index[None], value.shape)
+        return pltpu.roll(jnp.take_along_axis(value, index, axis=2), by, 1)
+
+    def update(k, low, high):
+        now, then = (even, odd) if k % 2 else (odd, even)
         rows = high - low
-        flat = (rows, 8, 128)
         top = min(high + 1, PAIRS)
         ext = now[(low - 1) * 16:top * 16].reshape(top - low + 1, 2, 8, 128)
         above = ext[0:rows]
@@ -254,21 +258,25 @@
             below = jnp.concatenate([ext[2:rows + 1], crossing], axis=0)
         else:
             below = ext[2:rows + 2]
-        left = pltpu.roll(jnp.take_along_axis(mid[:, 1], jnp.broadcast_to(index_left[None], flat), axis=2), 2, 1)
-        right = pltpu.roll(jnp.take_along_axis(mid[:, 0], jnp.broadcast_to(index_right[None], flat), axis=2), 6, 1)
+        left = shift(mid[:, 1], index_left, 2)
+        right = shift(mid[:, 0], index_right, 6)
         before = then[low * 16:high * 16].reshape(rows, 2, 8, 128)
         local = diag[low * 16:high * 16].reshape(rows, 2, 8, 128)
         parts = []
         for j, beside in enumerate((left + mid[:, 1], mid[:, 0] + right)):
             old = before[:, j]
-            if step == 1:
-                old = old * double
+            if k == 2:
+                old = old + old
             parts.append((local[:, j] * mid[:, j] - old) - scale * ((above[:, j] + below[:, j]) + beside))
         after = jnp.stack(parts, axis=1)
         then[low * 16:high * 16] = after.reshape(rows * 16, 128)
-        if accumulate:
-            term = (c_now * mid + c_next * after).reshape(rows * 16, 128)
-            filt[...] = filt[...] + term
+        if k % 2 == 0 and high == PAIRS:
+            first = max(ROWS, low)
+            c_now = coef[8 * k - 8:8 * k]
+            c_next = coef[8 * k:8 * k + 8]
+            term = c_now * mid[first - low:] + c_next * after[first - low:]
+            place_in = slice((first - ROWS) * 16, (PAIRS - ROWS) * 16)
+            filt[place_in] = filt[place_in] + term.reshape((PAIRS - first) * 16, 128)
 
     def vec_copy(q, j):
         peer = lax.rem(v + j, NV)
@@ -295,20 +303,12 @@
         filt[...] = (
             (2.0 * coef[0:8]) * even[16 * ROWS:16 * PAIRS].reshape(2 * (PAIRS - ROWS), 8, 128)
         ).reshape(16 * (PAIRS - ROWS), 128)
-        for block in range(4):
-            low = 8 * block + 1
-
-            def pair(i, inner, block=block, low=low):
-                k = 8 * block + 2 * i + 1
-                double = jnp.where(k == 1, 2.0, 1.0).astype(F32)
-                c_now = coef[pl.ds(pl.multiple_of(8 * k, 8), 8)]
-                c_next = coef[pl.ds(pl.multiple_of(8 * k + 8, 8), 8)]
-                for step in range(2):
-                    update(step, low, ROWS, double, None, None, False)
-                    update(step, ROWS, PAIRS, double, c_now, c_next, step == 1)
-                return inner
-
-            lax.fori_loop(0, 4, pair, 0)
+        for k in range(1, DEGREE + 1):
+            if k < ROWS - 1:
+                update(k, k, ROWS)
+                update(k, ROWS, PAIRS)
+            else:
+                update(k, k, PAIRS)
         for row in range(ROWS + 1):
             base, half = pair_place(ROWS + row)
             filtered[q, 8 * row:8 * row + 8] = filt[pl.ds(base - 16 * ROWS + half, 8, stride=2), :]
@@ -455,7 +455,7 @@
     ritz_shape = jax.ShapeDtypeStruct((NVEC, NVEC), F32)
     fields, ritz = pl.pallas_call(
         kernel,
-        out_shape=(jax.ShapeDtypeStruct((NQ, OWN, 128), F32), ritz_shape),
+        out_shape=(pltpu.VMEM((NQ, OWN, 128), F32), pltpu.VMEM((NVEC, NVEC), F32)),
         in_specs=[pl.BlockSpec(memory_space=pltpu.SMEM), hbm, hbm],
         out_specs=(vmem, vmem),
         scratch_shapes=[
@@ -482,7 +482,7 @@
             dma((3,)), dma((3,)), dma((1,)), dma((1,)),
         ],
         compiler_params=pltpu.CompilerParams(
-            collective_id=0, has_side_effects=True, vmem_limit_bytes=63 << 20
+            collective_id=0, has_side_effects=True, vmem_limit_bytes=60 << 20
         ),
         name="filter_ritz",
     )(bounds, start_vectors, potential)
@@ -492,7 +492,7 @@
         in_specs=[vmem, vmem],
         out_specs=(vmem, vmem),
         name="arrange",
-    )(fields, ritz)
+    )(pltpu.with_memory_space_constraint(fields, pltpu.VMEM), pltpu.with_memory_space_constraint(ritz, pltpu.VMEM))
 
 
 def solution(mesh):

time: 85.5 us -> 81.7 us (0.956)
  Pallas kernels: 84.7 us -> 81 us
    pallas_call x1, Pallas kernels: 82.8 us -> 80.1 us  [shards(): pl.pallas_call(kernel, out_shape=(pltpu.VMEM((NQ, OWN, 128), F32), pltpu....]
    pallas_call x1, Pallas kernels: 1.94 us -> 0.9 us  [shards(): pl.pallas_call(arrange, out_shape=(jax.ShapeDtypeStruct((NQ, ROWS, 1024),...]
where the time goes in v4:
time: 81.7 us; the launch traced here: 81.6 us
  Pallas kernels  81 us (99%)
    pallas_call x1, Pallas kernels, shards(): pl.pallas_call(kernel, out_shape=(pltpu.VMEM((NQ, OWN, 128), F32), pltpu....  80.1 us

profile of v4, /device:TPU:1, one launch (start us, length us, event | category | flops | bytes accessed | tf_op | source)
XLA Modules:
  0.0 81.6 jit_solution(17711922232450055224)
XLA Ops:
  0.6 80.1 %filter_ritz.1 = (f32[4,256,128]{2,1,0:T(8,128)S(1)}, f32[64,64]{1,0:T(8,128)S(1)}) custom-call(s32[4]{0:T(128)} %bounds_ref.1, f32[4,32,1024]{2,1,0:T(8,128)} %x_hbm.1, s32[32,1024]{1,0:T(8,128)} %pot_hbm.1), custom_call_target="tpu_custom_call" | custom-call | tf_op jit(solution)/shard_map/filter_ritz/pallas_call | solution.py:456
  80.7 0.9 %arrange.1 = (f32[4,32,1024]{2,1,0:T(8,128)}, f32[64,64]{1,0:T(8,128)}) custom-call(f32[4,256,128]{2,1,0:T(8,128)S(1)} %get-tuple-element.4.fields, f32[64,64]{1,0:T(8,128)S(1)} %get-tuple-element.5.ritz), custom_call_target="tpu_custom_call" | custom-call | tf_op jit(solution)/shard_map/arrange/pallas_call | solution.py:489

commit v5 on v4

--- a/solution.py
+++ b/solution.py
@@ -17,11 +17,16 @@
 PIECE = ROWS // NV
 SUB = 8
 CHUNKS = PIECE * SUB
-HALO = CHUNKS + SUB
 FIELD = (3 * ROWS + 1) * SUB
 PAIRS = 3 * ROWS // 2 + 1
-NA = 8
-NB = 32
+STRIP_STEPS = sorted(
+    ((a, b, c) for a in range(4) for b in range(2) for c in range(2) if a or b or c),
+    key=lambda step: -(2 * min(step[0], 4 - step[0]) + 2 * step[1] + step[2]),
+)
+VEC_STEPS = sorted(
+    ((a, b) for a in range(2) for b in range(8) if a or b), key=lambda step: -(2 * step[0] + min(step[1], 8 - step[1]))
+)
+PART = NVEC // NS
 OWN = ROWS * SUB
 HALF_PI = math.pi / 2
 SITES = NS * ROWS * 1024
@@ -124,23 +129,19 @@
 
 def kernel(
     bounds_ref, x_hbm, pot_hbm, fields, ritz_ref,
-    x_ref, pot_ref, coef, start, even, odd, filt, filtered, diag_rows, diag, pot_own, slab, ops, apply_ops,
-    gm, scattered, summed, total, ortho,
-    in_sem, pot_send, pot_recv, ghost_send, ghost_recv, vec_send, vec_recv, small_send, small_recv,
+    x_ref, pot_ref, coef, start, even, odd, filt, filtered, diag_rows, diag, pot_own, slab, halos, ops_y, ops_z, apply_ops,
+    parts, scattered, summed, total, ortho,
+    in_sem, pot_send, pot_recv, ghost_send, ghost_recv, vec_send, vec_recv, halo_send, halo_recv, small_send, small_recv,
     back_send, back_recv,
 ):
     s = lax.axis_index("strip")
     v = lax.axis_index("vec")
     y_lo = s // 2 % 2
-    along = s // 4 * 2 + s % 2
-    across = y_lo * NV + v
-    flipped = s + 2 - 4 * y_lo
 
     barrier = pltpu.get_barrier_semaphore()
 
     def greet(j, carry):
-        peer = lax.rem(v + j, NV)
-        for where in ({"strip": s, "vec": peer}, {"strip": flipped, "vec": peer}, {"strip": lax.rem(s + j, NS), "vec": v}):
+        for where in ({"vec": lax.rem(v + j, NV)}, {"strip": lax.rem(s + j, NS)}):
             pl.semaphore_signal(barrier, inc=1, device_id=where, device_id_type=pl.DeviceIdType.MESH)
         return carry
 
@@ -179,7 +180,7 @@
 
     classes_of(0, 0)
 
-    pl.semaphore_wait(barrier, 3 * (NV - 1))
+    pl.semaphore_wait(barrier, NV + NS - 2)
 
     up = lax.rem(s + NS - 1, NS)
     down = lax.rem(s + 1, NS)
@@ -228,8 +229,12 @@
     def pair_place(row):
         return (16 * row, 0) if row <= 48 else (16 * (96 - row), 1)
 
+    for copy in pot_copies() + ghost_copies(0):
+        copy.wait_send()
+    start_ghosts(1)
+
     for copy in pot_copies():
-        copy.wait()
+        copy.wait_recv()
     for row in range(1, 3 * ROWS):
         value = diag_rows[8 * row:8 * row + 8]
         for base, half in {pair_place(row), (16 * (96 - row), 1) if row == 48 else pair_place(row)}:
@@ -260,15 +265,17 @@
             below = ext[2:rows + 2]
         left = shift(mid[:, 1], index_left, 2)
         right = shift(mid[:, 0], index_right, 6)
-        before = then[low * 16:high * 16].reshape(rows, 2, 8, 128)
+        before = then[low * 16:high * 16].reshape(rows, 2, 8, 128) if k > 1 else None
         local = diag[low * 16:high * 16].reshape(rows, 2, 8, 128)
-        parts = []
+        halves = []
         for j, beside in enumerate((left + mid[:, 1], mid[:, 0] + right)):
-            old = before[:, j]
+            inside = local[:, j] * mid[:, j]
             if k == 2:
-                old = old + old
-            parts.append((local[:, j] * mid[:, j] - old) - scale * ((above[:, j] + below[:, j]) + beside))
-        after = jnp.stack(parts, axis=1)
+                inside = inside - (before[:, j] + before[:, j])
+            elif k > 2:
+                inside = inside - before[:, j]
+            halves.append(inside - scale * ((above[:, j] + below[:, j]) + beside))
+        after = jnp.stack(halves, axis=1)
         then[low * 16:high * 16] = after.reshape(rows * 16, 128)
         if k % 2 == 0 and high == PAIRS:
             first = max(ROWS, low)
@@ -281,25 +288,19 @@
     def vec_copy(q, j):
         peer = lax.rem(v + j, NV)
         return remote(
-            filtered.at[q, pl.ds(peer * CHUNKS, HALO)], slab.at[pl.ds((v * NQ + q) * HALO, HALO)],
+            filtered.at[q, pl.ds(peer * CHUNKS, CHUNKS)], slab.at[pl.ds((v * NQ + q) * CHUNKS, CHUNKS)],
             vec_send.at[q], vec_recv.at[q], vec=peer,
         )
 
     def one_vector(q, carry):
         for copy in ghost_copies(q):
-            copy.wait()
-
-        @pl.when(q < NQ - 1)
-        def _():
-            start_ghosts(q + 1)
-
+            copy.wait_recv()
         for row in range(3 * ROWS + 1):
             value = start[q, 8 * row:8 * row + 8]
             base, half = pair_place(row)
             even[pl.ds(base + half, 8, stride=2), :] = value
             if row == 48:
                 even[pl.ds(base + 1, 8, stride=2), :] = value
-        odd[...] = jnp.zeros((16 * PAIRS, 128), F32)
         filt[...] = (
             (2.0 * coef[0:8]) * even[16 * ROWS:16 * PAIRS].reshape(2 * (PAIRS - ROWS), 8, 128)
         ).reshape(16 * (PAIRS - ROWS), 128)
@@ -309,10 +310,17 @@
                 update(k, ROWS, PAIRS)
             else:
                 update(k, k, PAIRS)
+            if k == DEGREE // 2:
+                @pl.when(q < NQ - 2)
+                def _():
+                    for copy in ghost_copies(q + 1):
+                        copy.wait_send()
+                    start_ghosts(q + 2)
+
         for row in range(ROWS + 1):
             base, half = pair_place(ROWS + row)
             filtered[q, 8 * row:8 * row + 8] = filt[pl.ds(base - 16 * ROWS + half, 8, stride=2), :]
-        slab[pl.ds((v * NQ + q) * HALO, HALO)] = filtered[q, pl.ds(v * CHUNKS, HALO)]
+        slab[pl.ds((v * NQ + q) * CHUNKS, CHUNKS)] = filtered[q, pl.ds(v * CHUNKS, CHUNKS)]
 
         def send(j, inner):
             vec_copy(q, j).start()
@@ -322,20 +330,83 @@
         return carry
 
     lax.fori_loop(0, NQ, one_vector, 0)
+
+    def send_halos(j, carry):
+        peer = lax.rem(v + j, NV)
+        for q in range(NQ):
+            remote(
+                filtered.at[q, pl.ds(peer * CHUNKS + CHUNKS, SUB)], halos.at[pl.ds((v * NQ + q) * SUB, SUB)],
+                halo_send.at[0], halo_recv.at[0], vec=peer,
+            ).start()
+        return carry
+
+    lax.fori_loop(1, NV, send_halos, 0)
     for q in range(NQ):
-        wait_bytes(slab.at[pl.ds(0, (NV - 1) * HALO)], vec_recv.at[q])
-
-    lane16 = lax.broadcasted_iota(jnp.int32, (16, 128), 1)
+        halos[pl.ds((v * NQ + q) * SUB, SUB)] = filtered[q, pl.ds(v * CHUNKS + CHUNKS, SUB)]
+    for q in range(NQ):
+        wait_bytes(slab.at[pl.ds(0, (NV - 1) * CHUNKS)], vec_recv.at[q])
+
+    def take(source, stride, g, n):
+        base = 16 * g * stride + n
+        return jnp.concatenate(
+            [source[pl.ds(base, 8, stride=stride), :], source[pl.ds(base + 8 * stride, 8, stride=stride), :]], axis=0
+        )
+
+    def keep(target, g, n, value):
+        for part, half in enumerate(split(value)):
+            target[64 * part + 16 * g:64 * part + 16 * g + 16, 128 * n:128 * n + 128] = half
+
+    def matrix_part(left):
+        prod = lax.dot_general(left[...], ops_y[...], (((1,), (1,)), ((), ())), preferred_element_type=F32)
+        return prod[0:64] + prod[64:128]
+
+    def along_strip(stage, i, source, target):
+        for a, b, c in STRIP_STEPS:
+            peer = lax.rem(s // 4 + a, 4) * 4 + lax.rem(y_lo + b, 2) * 2 + lax.rem(s % 2 + c, 2)
+            remote(source(peer), target, small_send.at[i, stage], small_recv.at[i, stage], strip=peer).start()
+
+    def scatter(i, value):
+        for c in range(NS):
+            parts[i, c] = value[PART * c:PART * c + PART]
+        scattered[i, s] = parts[i, s]
+        along_strip(0, i, lambda peer: parts.at[i, peer], scattered.at[i, s])
+
+    def exchange(i):
+        wait_bytes(scattered.at[i, pl.ds(0, NS - 1)], small_recv.at[i, 0])
+        summed[i, v] = jnp.sum(scattered[i], axis=0)
+        for a, b in VEC_STEPS:
+            peer = lax.rem(v // 8 + a, 2) * 8 + lax.rem(v % 8 + b, 8)
+            remote(
+                summed.at[i, v], summed.at[i, v], small_send.at[i, 1], small_recv.at[i, 1], vec=peer
+            ).start()
+
+    def gather(i):
+        wait_bytes(summed.at[i, pl.ds(0, NV - 1)], small_recv.at[i, 1])
+        total[i, s] = jnp.sum(summed[i], axis=0)
+        along_strip(2, i, lambda peer: total.at[i, s], total.at[i, s])
+
+    def finish(i):
+        wait_bytes(total.at[i, pl.ds(0, NS - 1)], small_recv.at[i, 2])
+        value = jnp.concatenate([total[i, c] for c in range(NS)], axis=0)
+        return value + pltpu.roll(value, 64, 1)
+
+    for g in range(NVEC // 16):
+        for n in range(CHUNKS):
+            keep(ops_y, g, n, take(slab, CHUNKS, g, n))
+    scatter(0, matrix_part(ops_y))
+
+    for g in range(NVEC // 16):
+        for row in range(PIECE):
+            tiles = from_classes([take(slab, CHUNKS, g, SUB * row + place(c)) for c in range(SUB)])
+            for t, tile in enumerate(tiles):
+                keep(apply_ops, g, SUB * row + t, tile)
+    exchange(0)
+
+    wait_bytes(halos.at[pl.ds(0, (NV - 1) * NQ * SUB)], halo_recv.at[0])
     pot_slab = pot_own[pl.ds(v * CHUNKS, CHUNKS)] * 0.5
-
-    def chunk(g, n):
-        base = 16 * g * HALO + n
-        return jnp.concatenate(
-            [slab[pl.ds(base, 8, stride=HALO), :], slab[pl.ds(base + 8 * HALO, 8, stride=HALO), :]], axis=0
-        )
-
     for g in range(NVEC // 16):
-        y = [chunk(g, n) for n in range(HALO)]
+        y = [take(slab, CHUNKS, g, n) for n in range(CHUNKS)]
+        y += [take(halos, SUB, g, n) for n in range(SUB)]
         for row in range(PIECE):
             for c in range(SUB):
                 n = SUB * row + place(c)
@@ -343,60 +414,15 @@
                     right = y[SUB * row + place(c + 1)]
                 else:
                     right = pltpu.roll(y[SUB * row + place(0)], 127, 1)
-                z = pot_slab[n:n + 1] * y[n] - (right + y[n + SUB])
-                for part, value in enumerate(split(y[n]) + split(z)):
-                    ops[64 * part + 16 * g:64 * part + 16 * g + 16, 128 * n:128 * n + 128] = value
-    prod = lax.dot_general(
-        ops[...], ops[0:128, :], (((1,), (1,)), ((), ())), preferred_element_type=F32
-    )
+                keep(ops_z, g, n, pot_slab[n:n + 1] * y[n] - (right + y[n + SUB]))
+    scatter(1, matrix_part(ops_z))
+    gather(0)
+    exchange(1)
+
     rows64 = lax.broadcasted_iota(jnp.int32, (64, 128), 0)
     lanes64 = lax.broadcasted_iota(jnp.int32, (64, 128), 1)
-    gram_part = prod[0:64] + prod[64:128]
-    cross_part = prod[128:192] + prod[192:256]
-    gm[...] = jnp.where(
-        lanes64 < 64, gram_part + pltpu.roll(gram_part, 64, 1), cross_part + pltpu.roll(cross_part, 64, 1)
-    )
-
-    def to_along(stage, source, target):
-        def send(j, carry):
-            peer = lax.rem(along + j, NA)
-            strip = peer // 2 * 4 + y_lo * 2 + peer % 2
-            remote(source(peer), target, small_send.at[stage], small_recv.at[stage], strip=strip).start()
-            return carry
-
-        lax.fori_loop(1, NA, send, 0)
-
-    mine_a = pl.ds(along * 8, 8)
-    mine_b = pl.ds(across * 8, 8)
-    scattered[mine_a] = gm[mine_a]
-    to_along(0, lambda peer: gm.at[pl.ds(peer * 8, 8)], scattered.at[mine_a])
-
-    for g in range(NVEC // 16):
-        for row in range(PIECE):
-            tiles = from_classes([chunk(g, SUB * row + place(c)) for c in range(SUB)])
-            for t, tile in enumerate(tiles):
-                n = SUB * row + t
-                for part, value in enumerate(split(tile)):
-                    apply_ops[64 * part + 16 * g:64 * part + 16 * g + 16, 128 * n:128 * n + 128] = value
-
-    wait_bytes(scattered.at[pl.ds(0, 8 * (NA - 1))], small_recv.at[0])
-    summed[mine_b] = jnp.sum(scattered[...].reshape(NA, 8, 128), axis=0)
-
-    def send_across(j, carry):
-        peer = lax.rem(across + j, NB)
-        strip = s + 2 * (peer // NV - y_lo)
-        remote(
-            summed.at[mine_b], summed.at[mine_b], small_send.at[1], small_recv.at[1], strip=strip, vec=peer % NV
-        ).start()
-        return carry
-
-    lax.fori_loop(1, NB, send_across, 0)
-    wait_bytes(summed.at[pl.ds(0, 8 * (NB - 1))], small_recv.at[1])
-    total[mine_a] = jnp.sum(summed[...].reshape(NB, 8, 128), axis=0)
-    to_along(2, lambda peer: total.at[mine_a], total.at[mine_a])
-    wait_bytes(total.at[pl.ds(0, 8 * (NA - 1))], small_recv.at[2])
-
-    inverse = inverse_factor(jnp.where(lanes64 < 64, total[...], jnp.where(lanes64 - 64 == rows64, 1.0, 0.0)))
+    gram = finish(0)
+    inverse = inverse_factor(jnp.where(lanes64 < 64, gram, jnp.where(lanes64 - 64 == rows64, 1.0, 0.0)))
 
     high, low = split(math.sqrt(SITES) * inverse)
     left = jnp.concatenate(
@@ -424,7 +450,8 @@
     for q in range(NQ):
         fields[q, pl.ds(v * CHUNKS, CHUNKS)] = ortho[pl.ds((v * NQ + q) * CHUNKS, CHUNKS)]
 
-    cross = pltpu.roll(total[...], 64, 1)[:, 0:64]
+    gather(1)
+    cross = finish(1)[:, 0:64]
     cross = cross + cross.T
     half = jnp.dot(inverse, cross, precision=lax.Precision.HIGHEST, preferred_element_type=F32)
     ritz_ref[...] = float(ROWS) * lax.dot_general(
@@ -433,11 +460,14 @@
 
     wait_bytes(ortho.at[pl.ds(0, (NV - 1) * NQ * CHUNKS)], back_recv.at[0])
     wait_bytes(ortho.at[pl.ds(0, (NV - 1) * NQ * CHUNKS)], back_send.at[0])
-    wait_bytes(scattered.at[pl.ds(0, 8 * (NA - 1))], small_send.at[0])
-    wait_bytes(summed.at[pl.ds(0, 8 * (NB - 1))], small_send.at[1])
-    wait_bytes(scattered.at[pl.ds(0, 8 * (NA - 1))], small_send.at[2])
+    for i in range(2):
+        for stage in range(3):
+            wait_bytes(total.at[i, pl.ds(0, NS - 1)], small_send.at[i, stage])
+    wait_bytes(halos.at[pl.ds(0, (NV - 1) * NQ * SUB)], halo_send.at[0])
     for q in range(NQ):
-        wait_bytes(slab.at[pl.ds(0, (NV - 1) * HALO)], vec_send.at[q])
+        wait_bytes(slab.at[pl.ds(0, (NV - 1) * CHUNKS)], vec_send.at[q])
+    for copy in ghost_copies(NQ - 1):
+        copy.wait_send()
 
 
 def arrange(fields, ritz, out_ref, ritz_ref):
@@ -470,16 +500,18 @@
             pltpu.VMEM((FIELD, 128), F32),
             pltpu.VMEM((16 * PAIRS, 128), F32),
             pltpu.VMEM((OWN, 128), F32),
-            pltpu.VMEM((NVEC * HALO, 128), F32),
-            pltpu.VMEM((256, CHUNKS * 128), BF16),
+            pltpu.VMEM((NVEC * CHUNKS, 128), F32),
+            pltpu.VMEM((NVEC * SUB, 128), F32),
             pltpu.VMEM((128, CHUNKS * 128), BF16),
-            pltpu.VMEM((64, 128), F32),
-            pltpu.VMEM((8 * NA, 128), F32),
-            pltpu.VMEM((8 * NB, 128), F32),
-            pltpu.VMEM((64, 128), F32),
+            pltpu.VMEM((128, CHUNKS * 128), BF16),
+            pltpu.VMEM((128, CHUNKS * 128), BF16),
+            pltpu.VMEM((2, NS, PART, 128), F32),
+            pltpu.VMEM((2, NS, PART, 128), F32),
+            pltpu.VMEM((2, NV, PART, 128), F32),
+            pltpu.VMEM((2, NS, PART, 128), F32),
             pltpu.VMEM((NVEC * CHUNKS, 128), F32),
-            dma((2,)), dma((2,)), dma((2,)), dma((NQ, 3)), dma((NQ, 3)), dma((NQ,)), dma((NQ,)),
-            dma((3,)), dma((3,)), dma((1,)), dma((1,)),
+            dma((2,)), dma((2,)), dma((2,)), dma((NQ, 3)), dma((NQ, 3)), dma((NQ,)), dma((NQ,)), dma((1,)), dma((1,)),
+            dma((2, 3)), dma((2, 3)), dma((1,)), dma((1,)),
         ],
         compiler_params=pltpu.CompilerParams(
             collective_id=0, has_side_effects=True, vmem_limit_bytes=60 << 20

time: 81.7 us -> 78.4 us (0.960)
  Pallas kernels: 81 us -> 77.6 us
    pallas_call x1, Pallas kernels: 80.1 us -> 76.7 us  [shards(): pl.pallas_call(kernel, out_shape=(pltpu.VMEM((NQ, OWN, 128), F32), pltpu....]
where the time goes in v5:
time: 78.4 us; the launch traced here: 78.3 us
  Pallas kernels  77.6 us (99%)
    pallas_call x1, Pallas kernels, shards(): pl.pallas_call(kernel, out_shape=(pltpu.VMEM((NQ, OWN, 128), F32), pltpu....  76.7 us

profile of v5, /device:TPU:1, one launch (start us, length us, event | category | flops | bytes accessed | tf_op | source)
XLA Modules:
  0.0 78.3 jit_solution(7436539649114699335)
XLA Ops:
  0.6 76.7 %filter_ritz.1 = (f32[4,256,128]{2,1,0:T(8,128)S(1)}, f32[64,64]{1,0:T(8,128)S(1)}) custom-call(s32[4]{0:T(128)} %bounds_ref.1, f32[4,32,1024]{2,1,0:T(8,128)} %x_hbm.1, s32[32,1024]{1,0:T(8,128)} %pot_hbm.1), custom_call_target="tpu_custom_call" | custom-call | tf_op jit(solution)/shard_map/filter_ritz/pallas_call | solution.py:486
  77.4 0.9 %arrange.1 = (f32[4,32,1024]{2,1,0:T(8,128)}, f32[64,64]{1,0:T(8,128)}) custom-call(f32[4,256,128]{2,1,0:T(8,128)S(1)} %get-tuple-element.4.fields, f32[64,64]{1,0:T(8,128)S(1)} %get-tuple-element.5.ritz), custom_call_target="tpu_custom_call" | custom-call | tf_op jit(solution)/shard_map/arrange/pallas_call | solution.py:521

commit v6 on v5

--- a/solution.py
+++ b/solution.py
@@ -331,18 +331,18 @@
 
     lax.fori_loop(0, NQ, one_vector, 0)
 
+    wait_bytes(slab.at[pl.ds(0, (NV - 1) * CHUNKS)], vec_send.at[NQ - 1])
+
     def send_halos(j, carry):
         peer = lax.rem(v + j, NV)
-        for q in range(NQ):
-            remote(
-                filtered.at[q, pl.ds(peer * CHUNKS + CHUNKS, SUB)], halos.at[pl.ds((v * NQ + q) * SUB, SUB)],
-                halo_send.at[0], halo_recv.at[0], vec=peer,
-            ).start()
+        remote(
+            filtered.at[:, pl.ds(peer * CHUNKS + CHUNKS, SUB)], halos.at[pl.ds(v * NQ, NQ)],
+            halo_send.at[0], halo_recv.at[0], vec=peer,
+        ).start()
         return carry
 
     lax.fori_loop(1, NV, send_halos, 0)
-    for q in range(NQ):
-        halos[pl.ds((v * NQ + q) * SUB, SUB)] = filtered[q, pl.ds(v * CHUNKS + CHUNKS, SUB)]
+    halos[pl.ds(v * NQ, NQ)] = filtered[:, pl.ds(v * CHUNKS + CHUNKS, SUB)]
     for q in range(NQ):
         wait_bytes(slab.at[pl.ds(0, (NV - 1) * CHUNKS)], vec_recv.at[q])
 
@@ -402,11 +402,11 @@
                 keep(apply_ops, g, SUB * row + t, tile)
     exchange(0)
 
-    wait_bytes(halos.at[pl.ds(0, (NV - 1) * NQ * SUB)], halo_recv.at[0])
+    wait_bytes(halos.at[pl.ds(0, (NV - 1) * NQ)], halo_recv.at[0])
     pot_slab = pot_own[pl.ds(v * CHUNKS, CHUNKS)] * 0.5
     for g in range(NVEC // 16):
         y = [take(slab, CHUNKS, g, n) for n in range(CHUNKS)]
-        y += [take(halos, SUB, g, n) for n in range(SUB)]
+        y += [take(halos.reshape(NVEC * SUB, 128), SUB, g, n) for n in range(SUB)]
         for row in range(PIECE):
             for c in range(SUB):
                 n = SUB * row + place(c)
@@ -429,26 +429,22 @@
         [jnp.concatenate([high, high], axis=1), jnp.concatenate([low, low], axis=1)], axis=0
     )
     product = jnp.dot(left, apply_ops[...], preferred_element_type=F32)
+    flat = ortho.reshape(NVEC * CHUNKS, 128)
     for n in range(CHUNKS):
         value = product[0:64, 128 * n:128 * n + 128] + product[64:128, 128 * n:128 * n + 128]
         for g in range(8):
-            ortho[pl.ds(n + 8 * g * CHUNKS, 8, stride=CHUNKS), :] = value[8 * g:8 * g + 8]
-
-    def back_copy(j, q):
+            flat[pl.ds(n + 8 * g * CHUNKS, 8, stride=CHUNKS), :] = value[8 * g:8 * g + 8]
+
+    def send_back(j, carry):
         peer = lax.rem(v + j, NV)
-        return remote(
-            ortho.at[pl.ds((peer * NQ + q) * CHUNKS, CHUNKS)], fields.at[q, pl.ds(v * CHUNKS, CHUNKS)],
+        remote(
+            ortho.at[pl.ds(peer * NQ, NQ)], fields.at[:, pl.ds(v * CHUNKS, CHUNKS)],
             back_send.at[0], back_recv.at[0], vec=peer,
-        )
-
-    def send_back(j, carry):
-        for q in range(NQ):
-            back_copy(j, q).start()
+        ).start()
         return carry
 
     lax.fori_loop(1, NV, send_back, 0)
-    for q in range(NQ):
-        fields[q, pl.ds(v * CHUNKS, CHUNKS)] = ortho[pl.ds((v * NQ + q) * CHUNKS, CHUNKS)]
+    fields[:, pl.ds(v * CHUNKS, CHUNKS)] = ortho[pl.ds(v * NQ, NQ)]
 
     gather(1)
     cross = finish(1)[:, 0:64]
@@ -458,13 +454,13 @@
         inverse, half, (((1,), (1,)), ((), ())), precision=lax.Precision.HIGHEST, preferred_element_type=F32
     )
 
-    wait_bytes(ortho.at[pl.ds(0, (NV - 1) * NQ * CHUNKS)], back_recv.at[0])
-    wait_bytes(ortho.at[pl.ds(0, (NV - 1) * NQ * CHUNKS)], back_send.at[0])
+    wait_bytes(ortho.at[pl.ds(0, (NV - 1) * NQ)], back_recv.at[0])
+    wait_bytes(ortho.at[pl.ds(0, (NV - 1) * NQ)], back_send.at[0])
     for i in range(2):
         for stage in range(3):
             wait_bytes(total.at[i, pl.ds(0, NS - 1)], small_send.at[i, stage])
-    wait_bytes(halos.at[pl.ds(0, (NV - 1) * NQ * SUB)], halo_send.at[0])
-    for q in range(NQ):
+    wait_bytes(halos.at[pl.ds(0, (NV - 1) * NQ)], halo_send.at[0])
+    for q in range(NQ - 1):
         wait_bytes(slab.at[pl.ds(0, (NV - 1) * CHUNKS)], vec_send.at[q])
     for copy in ghost_copies(NQ - 1):
         copy.wait_send()
@@ -501,7 +497,7 @@
             pltpu.VMEM((16 * PAIRS, 128), F32),
             pltpu.VMEM((OWN, 128), F32),
             pltpu.VMEM((NVEC * CHUNKS, 128), F32),
-            pltpu.VMEM((NVEC * SUB, 128), F32),
+            pltpu.VMEM((NVEC, SUB, 128), F32),
             pltpu.VMEM((128, CHUNKS * 128), BF16),
             pltpu.VMEM((128, CHUNKS * 128), BF16),
             pltpu.VMEM((128, CHUNKS * 128), BF16),
@@ -509,7 +505,7 @@
             pltpu.VMEM((2, NS, PART, 128), F32),
             pltpu.VMEM((2, NV, PART, 128), F32),
             pltpu.VMEM((2, NS, PART, 128), F32),
-            pltpu.VMEM((NVEC * CHUNKS, 128), F32),
+            pltpu.VMEM((NVEC, CHUNKS, 128), F32),
             dma((2,)), dma((2,)), dma((2,)), dma((NQ, 3)), dma((NQ, 3)), dma((NQ,)), dma((NQ,)), dma((1,)), dma((1,)),
             dma((2, 3)), dma((2, 3)), dma((1,)), dma((1,)),
         ],

time: 78.4 us -> 78.7 us (level)
  no operation moved by 1% of the time
where the time goes in v6:
time: 78.7 us; the launch traced here: 78.5 us
  Pallas kernels  77.9 us (99%)
    pallas_call x1, Pallas kernels, shards(): pl.pallas_call(kernel, out_shape=(pltpu.VMEM((NQ, OWN, 128), F32), pltpu....  77 us

profile of v6, /device:TPU:1, one launch (start us, length us, event | category | flops | bytes accessed | tf_op | source)
XLA Modules:
  0.0 78.5 jit_solution(8222702907028580364)
XLA Ops:
  0.6 77.0 %filter_ritz.1 = (f32[4,256,128]{2,1,0:T(8,128)S(1)}, f32[64,64]{1,0:T(8,128)S(1)}) custom-call(s32[4]{0:T(128)} %bounds_ref.1, f32[4,32,1024]{2,1,0:T(8,128)} %x_hbm.1, s32[32,1024]{1,0:T(8,128)} %pot_hbm.1), custom_call_target="tpu_custom_call" | custom-call | tf_op jit(solution)/shard_map/filter_ritz/pallas_call | solution.py:482
  77.6 0.9 %arrange.1 = (f32[4,32,1024]{2,1,0:T(8,128)}, f32[64,64]{1,0:T(8,128)}) custom-call(f32[4,256,128]{2,1,0:T(8,128)S(1)} %get-tuple-element.4.fields, f32[64,64]{1,0:T(8,128)S(1)} %get-tuple-element.5.ritz), custom_call_target="tpu_custom_call" | custom-call | tf_op jit(solution)/shard_map/arrange/pallas_call | solution.py:517

commit v7 on v6

--- a/solution.py
+++ b/solution.py
@@ -17,6 +17,8 @@
 PIECE = ROWS // NV
 SUB = 8
 CHUNKS = PIECE * SUB
+HALO = CHUNKS + SUB
+LAST = NQ - 1
 FIELD = (3 * ROWS + 1) * SUB
 PAIRS = 3 * ROWS // 2 + 1
 STRIP_STEPS = sorted(
@@ -285,12 +287,16 @@
             place_in = slice((first - ROWS) * 16, (PAIRS - ROWS) * 16)
             filt[place_in] = filt[place_in] + term.reshape((PAIRS - first) * 16, 128)
 
-    def vec_copy(q, j):
-        peer = lax.rem(v + j, NV)
-        return remote(
-            filtered.at[q, pl.ds(peer * CHUNKS, CHUNKS)], slab.at[pl.ds((v * NQ + q) * CHUNKS, CHUNKS)],
-            vec_send.at[q], vec_recv.at[q], vec=peer,
-        )
+    def send_vector(q, count):
+        def send(j, carry):
+            peer = lax.rem(v + j, NV)
+            remote(
+                filtered.at[q, pl.ds(peer * CHUNKS, count)], slab.at[pl.ds((v * NQ + q) * HALO, count)],
+                vec_send.at[q], vec_recv.at[q], vec=peer,
+            ).start()
+            return carry
+
+        lax.fori_loop(1, NV, send, 0)
 
     def one_vector(q, carry):
         for copy in ghost_copies(q):
@@ -320,31 +326,21 @@
         for row in range(ROWS + 1):
             base, half = pair_place(ROWS + row)
             filtered[q, 8 * row:8 * row + 8] = filt[pl.ds(base - 16 * ROWS + half, 8, stride=2), :]
-        slab[pl.ds((v * NQ + q) * CHUNKS, CHUNKS)] = filtered[q, pl.ds(v * CHUNKS, CHUNKS)]
-
-        def send(j, inner):
-            vec_copy(q, j).start()
-            return inner
-
-        lax.fori_loop(1, NV, send, 0)
+        slab[pl.ds((v * NQ + q) * HALO, HALO)] = filtered[q, pl.ds(v * CHUNKS, HALO)]
+
+        @pl.when(q < LAST)
+        def _():
+            send_vector(q, HALO)
+
+        @pl.when(q == LAST)
+        def _():
+            send_vector(q, CHUNKS)
+
         return carry
 
     lax.fori_loop(0, NQ, one_vector, 0)
-
-    wait_bytes(slab.at[pl.ds(0, (NV - 1) * CHUNKS)], vec_send.at[NQ - 1])
-
-    def send_halos(j, carry):
-        peer = lax.rem(v + j, NV)
-        remote(
-            filtered.at[:, pl.ds(peer * CHUNKS + CHUNKS, SUB)], halos.at[pl.ds(v * NQ, NQ)],
-            halo_send.at[0], halo_recv.at[0], vec=peer,
-        ).start()
-        return carry
-
-    lax.fori_loop(1, NV, send_halos, 0)
-    halos[pl.ds(v * NQ, NQ)] = filtered[:, pl.ds(v * CHUNKS + CHUNKS, SUB)]
     for q in range(NQ):
-        wait_bytes(slab.at[pl.ds(0, (NV - 1) * CHUNKS)], vec_recv.at[q])
+        wait_bytes(slab.at[pl.ds(0, (NV - 1) * (CHUNKS if q == LAST else HALO))], vec_recv.at[q])
 
     def take(source, stride, g, n):
         base = 16 * g * stride + n
@@ -392,21 +388,33 @@
 
     for g in range(NVEC // 16):
         for n in range(CHUNKS):
-            keep(ops_y, g, n, take(slab, CHUNKS, g, n))
+            keep(ops_y, g, n, take(slab, HALO, g, n))
     scatter(0, matrix_part(ops_y))
+
+    def send_halos(j, carry):
+        peer = lax.rem(v + j, NV)
+        remote(
+            filtered.at[LAST, pl.ds(peer * CHUNKS + CHUNKS, SUB)], halos.at[v], halo_send.at[0], halo_recv.at[0], vec=peer
+        ).start()
+        return carry
+
+    lax.fori_loop(1, NV, send_halos, 0)
+    halos[v] = filtered[LAST, pl.ds(v * CHUNKS + CHUNKS, SUB)]
 
     for g in range(NVEC // 16):
         for row in range(PIECE):
-            tiles = from_classes([take(slab, CHUNKS, g, SUB * row + place(c)) for c in range(SUB)])
+            tiles = from_classes([take(slab, HALO, g, SUB * row + place(c)) for c in range(SUB)])
             for t, tile in enumerate(tiles):
                 keep(apply_ops, g, SUB * row + t, tile)
     exchange(0)
 
-    wait_bytes(halos.at[pl.ds(0, (NV - 1) * NQ)], halo_recv.at[0])
+    wait_bytes(halos.at[pl.ds(0, NV - 1)], halo_recv.at[0])
+    for peer in range(NV):
+        base = (peer * NQ + LAST) * HALO + CHUNKS
+        slab[base:base + SUB] = halos[peer]
     pot_slab = pot_own[pl.ds(v * CHUNKS, CHUNKS)] * 0.5
     for g in range(NVEC // 16):
-        y = [take(slab, CHUNKS, g, n) for n in range(CHUNKS)]
-        y += [take(halos.reshape(NVEC * SUB, 128), SUB, g, n) for n in range(SUB)]
+        y = [take(slab, HALO, g, n) for n in range(HALO)]
         for row in range(PIECE):
             for c in range(SUB):
                 n = SUB * row + place(c)
@@ -459,9 +467,9 @@
     for i in range(2):
         for stage in range(3):
             wait_bytes(total.at[i, pl.ds(0, NS - 1)], small_send.at[i, stage])
-    wait_bytes(halos.at[pl.ds(0, (NV - 1) * NQ)], halo_send.at[0])
-    for q in range(NQ - 1):
-        wait_bytes(slab.at[pl.ds(0, (NV - 1) * CHUNKS)], vec_send.at[q])
+    wait_bytes(halos.at[pl.ds(0, NV - 1)], halo_send.at[0])
+    for q in range(NQ):
+        wait_bytes(slab.at[pl.ds(0, (NV - 1) * (CHUNKS if q == LAST else HALO))], vec_send.at[q])
     for copy in ghost_copies(NQ - 1):
         copy.wait_send()
 
@@ -496,8 +504,8 @@
             pltpu.VMEM((FIELD, 128), F32),
             pltpu.VMEM((16 * PAIRS, 128), F32),
             pltpu.VMEM((OWN, 128), F32),
-            pltpu.VMEM((NVEC * CHUNKS, 128), F32),
-            pltpu.VMEM((NVEC, SUB, 128), F32),
+            pltpu.VMEM((NVEC * HALO, 128), F32),
+            pltpu.VMEM((NV, SUB, 128), F32),
             pltpu.VMEM((128, CHUNKS * 128), BF16),
             pltpu.VMEM((128, CHUNKS * 128), BF16),
             pltpu.VMEM((128, CHUNKS * 128), BF16),

time: 78.7 us -> 78.1 us (level)
  no operation moved by 1% of the time
where the time goes in v7:
time: 78.1 us; the launch traced here: 78 us
  Pallas kernels  77.4 us (99%)
    pallas_call x1, Pallas kernels, shards(): pl.pallas_call(kernel, out_shape=(pltpu.VMEM((NQ, OWN, 128), F32), pltpu....  76.5 us

profile of v7, /device:TPU:1, one launch (start us, length us, event | category | flops | bytes accessed | tf_op | source)
XLA Modules:
  0.0 78.0 jit_solution(12866467969368929092)
XLA Ops:
  0.6 76.5 %filter_ritz.1 = (f32[4,256,128]{2,1,0:T(8,128)S(1)}, f32[64,64]{1,0:T(8,128)S(1)}) custom-call(s32[4]{0:T(128)} %bounds_ref.1, f32[4,32,1024]{2,1,0:T(8,128)} %x_hbm.1, s32[32,1024]{1,0:T(8,128)} %pot_hbm.1), custom_call_target="tpu_custom_call" | custom-call | tf_op jit(solution)/shard_map/filter_ritz/pallas_call | solution.py:490
  77.1 0.9 %arrange.1 = (f32[4,32,1024]{2,1,0:T(8,128)}, f32[64,64]{1,0:T(8,128)}) custom-call(f32[4,256,128]{2,1,0:T(8,128)S(1)} %get-tuple-element.4.fields, f32[64,64]{1,0:T(8,128)S(1)} %get-tuple-element.5.ritz), custom_call_target="tpu_custom_call" | custom-call | tf_op jit(solution)/shard_map/arrange/pallas_call | solution.py:525

commit v8 on v7

--- a/solution.py
+++ b/solution.py
@@ -98,15 +98,14 @@
     return [jnp.take_along_axis(tile, index, axis=1) for tile in turn_blocks(tiles)]
 
 
-def inverse_factor(aug):
-    rows = [aug[8 * i:8 * i + 8] for i in range(8)]
+def eliminate(rows, panels):
     sub = lax.broadcasted_iota(jnp.int32, (8, 128), 0)
     done = []
 
     def spread(value, k):
         return jnp.broadcast_to(value[k:k + 1], (8, 128))
 
-    for p in range(8):
+    for p in panels:
         columns = {
             (j, i): jnp.broadcast_to(rows[i][:, 8 * p + j:8 * p + j + 1], (8, 128))
             for i in range(p, 8) for j in range(8)
@@ -132,7 +131,7 @@
 def kernel(
     bounds_ref, x_hbm, pot_hbm, fields, ritz_ref,
     x_ref, pot_ref, coef, start, even, odd, filt, filtered, diag_rows, diag, pot_own, slab, halos, ops_y, ops_z, apply_ops,
-    parts, scattered, summed, total, ortho,
+    parts, scattered, summed, total, ortho_first, ortho_second,
     in_sem, pot_send, pot_recv, ghost_send, ghost_recv, vec_send, vec_recv, halo_send, halo_recv, small_send, small_recv,
     back_send, back_recv,
 ):
@@ -430,29 +429,43 @@
     rows64 = lax.broadcasted_iota(jnp.int32, (64, 128), 0)
     lanes64 = lax.broadcasted_iota(jnp.int32, (64, 128), 1)
     gram = finish(0)
-    inverse = inverse_factor(jnp.where(lanes64 < 64, gram, jnp.where(lanes64 - 64 == rows64, 1.0, 0.0)))
-
-    high, low = split(math.sqrt(SITES) * inverse)
-    left = jnp.concatenate(
-        [jnp.concatenate([high, high], axis=1), jnp.concatenate([low, low], axis=1)], axis=0
-    )
-    product = jnp.dot(left, apply_ops[...], preferred_element_type=F32)
-    flat = ortho.reshape(NVEC * CHUNKS, 128)
-    for n in range(CHUNKS):
-        value = product[0:64, 128 * n:128 * n + 128] + product[64:128, 128 * n:128 * n + 128]
-        for g in range(8):
-            flat[pl.ds(n + 8 * g * CHUNKS, 8, stride=CHUNKS), :] = value[8 * g:8 * g + 8]
-
-    def send_back(j, carry):
-        peer = lax.rem(v + j, NV)
-        remote(
-            ortho.at[pl.ds(peer * NQ, NQ)], fields.at[:, pl.ds(v * CHUNKS, CHUNKS)],
-            back_send.at[0], back_recv.at[0], vec=peer,
-        ).start()
-        return carry
-
-    lax.fori_loop(1, NV, send_back, 0)
-    fields[:, pl.ds(v * CHUNKS, CHUNKS)] = ortho[pl.ds(v * NQ, NQ)]
+    aug = jnp.where(lanes64 < 64, gram, jnp.where(lanes64 - 64 == rows64, 1.0, 0.0))
+    aug_rows = [aug[8 * i:8 * i + 8] for i in range(8)]
+
+    blocks = []
+    for half, ortho in enumerate((ortho_first, ortho_second)):
+        block = eliminate(aug_rows, range(4 * half, 4 * half + 4))
+        blocks.append(block)
+        high, low = split(math.sqrt(SITES) * block)
+        left = jnp.concatenate(
+            [jnp.concatenate([high, high], axis=1), jnp.concatenate([low, low], axis=1)], axis=0
+        )
+        product = jnp.dot(left, apply_ops[...], preferred_element_type=F32)
+        flat = ortho.reshape(NVEC // 2 * CHUNKS, 128)
+        for n in range(CHUNKS):
+            value = product[0:32, 128 * n:128 * n + 128] + product[32:64, 128 * n:128 * n + 128]
+            for g in range(4):
+                flat[pl.ds(n + 8 * g * CHUNKS, 8, stride=CHUNKS), :] = value[8 * g:8 * g + 8]
+
+        def send_back(j, carry, half=half, ortho=ortho):
+            local = lax.rem(v + j, NV // 2)
+            peer = local + half * (NV // 2)
+
+            @pl.when(peer != v)
+            def _():
+                remote(
+                    ortho.at[pl.ds(local * NQ, NQ)], fields.at[:, pl.ds(v * CHUNKS, CHUNKS)],
+                    back_send.at[0], back_recv.at[0], vec=peer,
+                ).start()
+
+            @pl.when(peer == v)
+            def _():
+                fields[:, pl.ds(v * CHUNKS, CHUNKS)] = ortho[pl.ds(local * NQ, NQ)]
+
+            return carry
+
+        lax.fori_loop(0, NV // 2, send_back, 0)
+    inverse = jnp.concatenate(blocks, axis=0)
 
     gather(1)
     cross = finish(1)[:, 0:64]
@@ -462,8 +475,8 @@
         inverse, half, (((1,), (1,)), ((), ())), precision=lax.Precision.HIGHEST, preferred_element_type=F32
     )
 
-    wait_bytes(ortho.at[pl.ds(0, (NV - 1) * NQ)], back_recv.at[0])
-    wait_bytes(ortho.at[pl.ds(0, (NV - 1) * NQ)], back_send.at[0])
+    wait_bytes(slab.at[pl.ds(0, (NV - 1) * NQ * CHUNKS)], back_recv.at[0])
+    wait_bytes(slab.at[pl.ds(0, (NV - 1) * NQ * CHUNKS)], back_send.at[0])
     for i in range(2):
         for stage in range(3):
             wait_bytes(total.at[i, pl.ds(0, NS - 1)], small_send.at[i, stage])
@@ -513,7 +526,8 @@
             pltpu.VMEM((2, NS, PART, 128), F32),
             pltpu.VMEM((2, NV, PART, 128), F32),
             pltpu.VMEM((2, NS, PART, 128), F32),
-            pltpu.VMEM((NVEC, CHUNKS, 128), F32),
+            pltpu.VMEM((NVEC // 2, CHUNKS, 128), F32),
+            pltpu.VMEM((NVEC // 2, CHUNKS, 128), F32),
             dma((2,)), dma((2,)), dma((2,)), dma((NQ, 3)), dma((NQ, 3)), dma((NQ,)), dma((NQ,)), dma((1,)), dma((1,)),
             dma((2, 3)), dma((2, 3)), dma((1,)), dma((1,)),
         ],

time: 78.1 us -> 77.1 us (0.987)
  the two profiles are of different devices: /device:TPU:1 before, /device:TPU:24 now
where the time goes in v8:
time: 77.1 us; the launch traced here: 77 us
  Pallas kernels  76.4 us (99%)
    pallas_call x1, Pallas kernels, shards(): pl.pallas_call(kernel, out_shape=(pltpu.VMEM((NQ, OWN, 128), F32), pltpu....  75.5 us

profile of v8, /device:TPU:24, one launch (start us, length us, event | category | flops | bytes accessed | tf_op | source)
XLA Modules:
  0.0 77.0 jit_solution(16437125712157454105)
XLA Ops:
  0.6 75.5 %filter_ritz.1 = (f32[4,256,128]{2,1,0:T(8,128)S(1)}, f32[64,64]{1,0:T(8,128)S(1)}) custom-call(s32[4]{0:T(128)} %bounds_ref.1, f32[4,32,1024]{2,1,0:T(8,128)} %x_hbm.1, s32[32,1024]{1,0:T(8,128)} %pot_hbm.1), custom_call_target="tpu_custom_call" | custom-call | tf_op jit(solution)/shard_map/filter_ritz/pallas_call | solution.py:503
  76.1 0.9 %arrange.1 = (f32[4,32,1024]{2,1,0:T(8,128)}, f32[64,64]{1,0:T(8,128)}) custom-call(f32[4,256,128]{2,1,0:T(8,128)S(1)} %get-tuple-element.4.fields, f32[64,64]{1,0:T(8,128)S(1)} %get-tuple-element.5.ritz), custom_call_target="tpu_custom_call" | custom-call | tf_op jit(solution)/shard_map/arrange/pallas_call | solution.py:539

commit v9 on v8

--- a/solution.py
+++ b/solution.py
@@ -286,16 +286,16 @@
             place_in = slice((first - ROWS) * 16, (PAIRS - ROWS) * 16)
             filt[place_in] = filt[place_in] + term.reshape((PAIRS - first) * 16, 128)
 
+    def vec_peer(step):
+        return lax.rem(v // 8 + step[0], 2) * 8 + lax.rem(v % 8 + step[1], 8)
+
     def send_vector(q, count):
-        def send(j, carry):
-            peer = lax.rem(v + j, NV)
+        for step in VEC_STEPS:
+            peer = vec_peer(step)
             remote(
                 filtered.at[q, pl.ds(peer * CHUNKS, count)], slab.at[pl.ds((v * NQ + q) * HALO, count)],
                 vec_send.at[q], vec_recv.at[q], vec=peer,
             ).start()
-            return carry
-
-        lax.fori_loop(1, NV, send, 0)
 
     def one_vector(q, carry):
         for copy in ghost_copies(q):
@@ -369,10 +369,9 @@
     def exchange(i):
         wait_bytes(scattered.at[i, pl.ds(0, NS - 1)], small_recv.at[i, 0])
         summed[i, v] = jnp.sum(scattered[i], axis=0)
-        for a, b in VEC_STEPS:
-            peer = lax.rem(v // 8 + a, 2) * 8 + lax.rem(v % 8 + b, 8)
+        for step in VEC_STEPS:
             remote(
-                summed.at[i, v], summed.at[i, v], small_send.at[i, 1], small_recv.at[i, 1], vec=peer
+                summed.at[i, v], summed.at[i, v], small_send.at[i, 1], small_recv.at[i, 1], vec=vec_peer(step)
             ).start()
 
     def gather(i):
@@ -488,10 +487,10 @@
 
 
 def arrange(fields, ritz, out_ref, ritz_ref):
-    for q in range(NQ):
-        for r in range(ROWS // 8):
-            for t in range(SUB):
-                out_ref[q, 8 * r:8 * r + 8, 128 * t:128 * t + 128] = fields[q, pl.ds(64 * r + t, 8, stride=8), :]
+    q = pl.program_id(0)
+    for r in range(ROWS // 8):
+        for t in range(SUB):
+            out_ref[0, 8 * r:8 * r + 8, 128 * t:128 * t + 128] = fields[q, pl.ds(64 * r + t, 8, stride=8), :]
     ritz_ref[...] = ritz[...]
 
 
@@ -539,8 +538,9 @@
     return pl.pallas_call(
         arrange,
         out_shape=(jax.ShapeDtypeStruct((NQ, ROWS, 1024), F32), ritz_shape),
+        grid=(NQ,),
         in_specs=[vmem, vmem],
-        out_specs=(vmem, vmem),
+        out_specs=(pl.BlockSpec((1, ROWS, 1024), lambda q: (q, 0, 0)), pl.BlockSpec((NVEC, NVEC), lambda q: (0, 0))),
         name="arrange",
     )(pltpu.with_memory_space_constraint(fields, pltpu.VMEM), pltpu.with_memory_space_constraint(ritz, pltpu.VMEM))
 

time: 77.1 us -> 76.5 us (level)
    pallas_call x1, Pallas kernels: 75.5 us -> 74.3 us  [shards(): pl.pallas_call(kernel, out_shape=(pltpu.VMEM((NQ, OWN, 128), F32), pltpu....]
where the time goes in v9:
time: 76.5 us; the launch traced here: 76.4 us
  Pallas kernels  75.7 us (99%)
    pallas_call x1, Pallas kernels, shards(): pl.pallas_call(kernel, out_shape=(pltpu.VMEM((NQ, OWN, 128), F32), pltpu....  74.3 us

profile of v9, /device:TPU:24, one launch (start us, length us, event | category | flops | bytes accessed | tf_op | source)
XLA Modules:
  0.0 76.4 jit_solution(8558889809537121550)
XLA Ops:
  0.6 74.3 %filter_ritz.1 = (f32[4,256,128]{2,1,0:T(8,128)S(1)}, f32[64,64]{1,0:T(8,128)S(1)}) custom-call(s32[4]{0:T(128)} %bounds_ref.1, f32[4,32,1024]{2,1,0:T(8,128)} %x_hbm.1, s32[32,1024]{1,0:T(8,128)} %pot_hbm.1), custom_call_target="tpu_custom_call" | custom-call | tf_op jit(solution)/shard_map/filter_ritz/pallas_call | solution.py:502
  74.9 1.4 %arrange.1 = (f32[4,32,1024]{2,1,0:T(8,128)}, f32[64,64]{1,0:T(8,128)}) custom-call(f32[4,256,128]{2,1,0:T(8,128)S(1)} %get-tuple-element.4.fields, f32[64,64]{1,0:T(8,128)S(1)} %get-tuple-element.5.ritz), custom_call_target="tpu_custom_call" | custom-call | tf_op jit(solution)/shard_map/arrange/pallas_call | solution.py:538

commit v10 on v9

--- a/solution.py
+++ b/solution.py
@@ -487,10 +487,10 @@
 
 
 def arrange(fields, ritz, out_ref, ritz_ref):
-    q = pl.program_id(0)
-    for r in range(ROWS // 8):
-        for t in range(SUB):
-            out_ref[0, 8 * r:8 * r + 8, 128 * t:128 * t + 128] = fields[q, pl.ds(64 * r + t, 8, stride=8), :]
+    for q in range(NQ):
+        for r in range(ROWS // 8):
+            for t in range(SUB):
+                out_ref[q, 8 * r:8 * r + 8, 128 * t:128 * t + 128] = fields[q, pl.ds(64 * r + t, 8, stride=8), :]
     ritz_ref[...] = ritz[...]
 
 
@@ -538,9 +538,8 @@
     return pl.pallas_call(
         arrange,
         out_shape=(jax.ShapeDtypeStruct((NQ, ROWS, 1024), F32), ritz_shape),
-        grid=(NQ,),
         in_specs=[vmem, vmem],
-        out_specs=(pl.BlockSpec((1, ROWS, 1024), lambda q: (q, 0, 0)), pl.BlockSpec((NVEC, NVEC), lambda q: (0, 0))),
+        out_specs=(vmem, vmem),
         name="arrange",
     )(pltpu.with_memory_space_constraint(fields, pltpu.VMEM), pltpu.with_memory_space_constraint(ritz, pltpu.VMEM))
 

time: 76.5 us -> 75.9 us (level)
  no operation moved by 1% of the time
where the time goes in v10:
time: 75.9 us; the launch traced here: 75.8 us
  Pallas kernels  75.2 us (99%)
    pallas_call x1, Pallas kernels, shards(): pl.pallas_call(kernel, out_shape=(pltpu.VMEM((NQ, OWN, 128), F32), pltpu....  74.3 us

profile of v10, /device:TPU:24, one launch (start us, length us, event | category | flops | bytes accessed | tf_op | source)
XLA Modules:
  0.0 75.8 jit_solution(507755259704971054)
XLA Ops:
  0.6 74.3 %filter_ritz.1 = (f32[4,256,128]{2,1,0:T(8,128)S(1)}, f32[64,64]{1,0:T(8,128)S(1)}) custom-call(s32[4]{0:T(128)} %bounds_ref.1, f32[4,32,1024]{2,1,0:T(8,128)} %x_hbm.1, s32[32,1024]{1,0:T(8,128)} %pot_hbm.1), custom_call_target="tpu_custom_call" | custom-call | tf_op jit(solution)/shard_map/filter_ritz/pallas_call | solution.py:502
  74.9 0.9 %arrange.1 = (f32[4,32,1024]{2,1,0:T(8,128)}, f32[64,64]{1,0:T(8,128)}) custom-call(f32[4,256,128]{2,1,0:T(8,128)S(1)} %get-tuple-element.4.fields, f32[64,64]{1,0:T(8,128)S(1)} %get-tuple-element.5.ritz), custom_call_target="tpu_custom_call" | custom-call | tf_op jit(solution)/shard_map/arrange/pallas_call | solution.py:538
